TPU v7x, 32 devices: a whole 2x2x4 slice. The times are simulated.
32 devices in a mesh: section: 4 (over y, core), tensor: 8 (over z, x).
Axes of the slice: x: 2, y: 2, z: 4, core: 2. Of those that a mesh axis runs over, the one named last changes fastest.
Arguments:
- resid: bfloat16 [32, 4608], P('section', 'tensor'), may hold values from -6 to 6
- pre_gain: float32 [4, 4608], P('section'), may hold values from 0.5 to 1.5
- post_gain: float32 [4, 4608], P('section'), may hold values from 0.5 to 1.5
- w_query: bfloat16 [4, 4608, 4096], P('section', None, 'tensor'), may hold values from -0.09375 to 0.09375
- w_key: bfloat16 [4, 4608, 2048], P('section', None, 'tensor'), may hold values from -0.09375 to 0.09375
- w_value: bfloat16 [4, 4608, 2048], P('section', None, 'tensor'), may hold values from -0.09375 to 0.09375
- w_out: bfloat16 [4, 4096, 4608], P('section', 'tensor'), may hold values from -0.09375 to 0.09375
- key_cache: bfloat16 [4, 32, 16, 64, 128], P('section', None, 'tensor'), may hold values from -6 to 6
- value_cache: bfloat16 [4, 32, 16, 64, 128], P('section', None, 'tensor'), may hold values from -6 to 6
- lengths: int32 [32], replicated, may hold values from 1 to 64, as said below
- concept: int32 [32], replicated, may hold values from 0 to 511
- steer_layer: int32 [32], replicated, may hold values from 0 to 3
- strength: float32 [32], replicated, may hold values from 0.5 to 2
- directions: bfloat16 [512, 4608], P(None, 'tensor'), may hold values from -6 to 6
Outputs:
- final_resid: bfloat16 [32, 4608], P('section', 'tensor')
Inputs may be any that keep to these rules, and one draw needn't show every extreme that they name: `lengths`: some row of every draw has exactly 64.
All inputs are finite; a program needn't handle non-finite values.
Results may differ from a plain program's by a relative error of at most 0.03.
Values may be sent and summed in bfloat16 or wider, within the bound.
A program may use at most 64 MiB of HBM per device.

v0:
```python
import jax
import jax.numpy as jnp
from jax import lax
from jax.sharding import PartitionSpec as P

D = 4608
HEADS = 32
KVH = 16
HD = 128


epsilon = 1e-06
softcap_limit = 50.0


def from_behind(value, axis, steps):
    count = lax.axis_size(axis)
    pairs = [(source, (source + steps) % count) for source in range(count)]
    return lax.ppermute(value, axis, pairs)


def rotate(vectors, places):
    half_dim = vectors.shape[-1] // 2
    frequency = 10000.0 ** (-(jnp.arange(half_dim, dtype=jnp.float32) * 2.0) / vectors.shape[-1])
    angles = places[:, None, None] * frequency[None, None, :]
    first = vectors[..., :half_dim]
    second = vectors[..., half_dim:]
    cosine = jnp.cos(angles)
    sine = jnp.sin(angles)
    return jnp.concatenate(
        [first * cosine - second * sine, second * cosine + first * sine], axis=-1
    )


def attend(queries, new_keys, new_values, cache_keys, cache_values, row_lengths, scale):
    scores = (
        jnp.einsum("rkgd,rkcd->rkgc", queries, cache_keys, preferred_element_type=jnp.float32)
        * scale
    )
    own_score = (
        jnp.einsum("rkgd,rkd->rkg", queries, new_keys, preferred_element_type=jnp.float32) * scale
    )
    capped = softcap_limit * jnp.tanh(scores / softcap_limit)
    own_capped = softcap_limit * jnp.tanh(own_score / softcap_limit)
    valid = jnp.arange(cache_keys.shape[2], dtype=jnp.int32)[None, :] < row_lengths[:, None]
    weights = jnp.where(valid[:, None, None, :], jnp.exp(capped - softcap_limit), jnp.float32(0.0))
    own_weight = jnp.exp(own_capped - softcap_limit)
    totals = jnp.sum(weights, axis=-1) + own_weight
    probs = (weights / totals[..., None]).astype(jnp.bfloat16)
    own_prob = (own_weight / totals).astype(jnp.bfloat16)
    mixed = jnp.einsum("rkgc,rkcd->rkgd", probs, cache_values, preferred_element_type=jnp.float32)
    return (
        mixed
        + own_prob.astype(jnp.float32)[..., None] * new_values.astype(jnp.float32)[:, :, None, :]
    )


def on_device(
    resid,
    pre_gain,
    post_gain,
    w_query,
    w_key,
    w_value,
    w_out,
    key_cache,
    value_cache,
    lengths,
    concept,
    steer_layer,
    strength,
    directions,
):
    section_count = lax.axis_size("section")
    section_index = lax.axis_index("section")
    tensor_index = lax.axis_index("tensor")
    row_count = resid.shape[0]
    piece_width = resid.shape[1]
    group = HEADS // KVH
    local_kv = key_cache.shape[2]
    local_heads = local_kv * group
    scale = float(D // HEADS) ** (-0.5)
    pre_scale = pre_gain[0]
    post_scale = post_gain[0]
    query_weight = w_query[0]
    key_weight = w_key[0]
    value_weight = w_value[0]
    out_weight = w_out[0]
    layer_keys = key_cache[0]
    layer_values = value_cache[0]
    concept_ids = jnp.arange(directions.shape[0], dtype=jnp.int32)

    def advance(tick, current):
        batch_index = (section_index - tick) % section_count
        start_tick = tick - section_index
        active = (start_tick >= 0) & (start_tick < section_count)
        first_row = batch_index * row_count
        row_lengths = lax.dynamic_slice_in_dim(lengths, first_row, row_count, 0)
        row_concepts = lax.dynamic_slice_in_dim(concept, first_row, row_count, 0)
        row_steer = lax.dynamic_slice_in_dim(steer_layer, first_row, row_count, 0)
        row_strength = lax.dynamic_slice_in_dim(strength, first_row, row_count, 0)
        cache_keys = lax.dynamic_slice_in_dim(layer_keys, first_row, row_count, 0)
        cache_values = lax.dynamic_slice_in_dim(layer_values, first_row, row_count, 0)
        places = row_lengths.astype(jnp.float32)
        features = lax.all_gather(current, "tensor", axis=1, tiled=True)
        values_full = features.astype(jnp.float32)
        normed = (
            values_full
            * lax.rsqrt(jnp.mean(values_full * values_full, axis=-1, keepdims=True) + epsilon)
            * pre_scale
        ).astype(jnp.bfloat16)
        queries = rotate(
            jnp.dot(normed, query_weight, preferred_element_type=jnp.float32).reshape(
                row_count, local_heads, HD
            ),
            places,
        ).astype(jnp.bfloat16)
        new_keys = rotate(
            jnp.dot(normed, key_weight, preferred_element_type=jnp.float32).reshape(
                row_count, local_kv, HD
            ),
            places,
        ).astype(jnp.bfloat16)
        new_values = (
            jnp.dot(normed, value_weight, preferred_element_type=jnp.float32)
            .astype(jnp.bfloat16)
            .reshape(row_count, local_kv, HD)
        )
        mixed = attend(
            queries.reshape(row_count, local_kv, group, HD),
            new_keys,
            new_values,
            cache_keys,
            cache_values,
            row_lengths,
            scale,
        )
        heads_out = mixed.reshape(row_count, local_heads * HD).astype(jnp.bfloat16)
        partial_sum = jnp.dot(heads_out, out_weight, preferred_element_type=jnp.float32)
        summed = lax.psum(partial_sum.astype(jnp.bfloat16), "tensor").astype(jnp.float32)
        post_full = (
            summed
            * lax.rsqrt(jnp.mean(summed * summed, axis=-1, keepdims=True) + epsilon)
            * post_scale
        )
        post = lax.dynamic_slice_in_dim(post_full, tensor_index * piece_width, piece_width, 1)
        one_hot = (row_concepts[:, None] == concept_ids[None, :]).astype(jnp.bfloat16)
        steer_piece = jnp.dot(one_hot, directions, preferred_element_type=jnp.float32)
        steer_gate = row_strength * (row_steer == section_index).astype(jnp.float32)
        new_state = (current.astype(jnp.float32) + post + steer_gate[:, None] * steer_piece).astype(
            jnp.bfloat16
        )
        updated = jnp.where(active, new_state, current)
        return from_behind(updated, "section", 1)

    return lax.fori_loop(0, 2 * section_count, advance, resid)


def solution(mesh):
    placed = (
        P("section", "tensor"),
        P("section", None),
        P("section", None),
        P("section", None, "tensor"),
        P("section", None, "tensor"),
        P("section", None, "tensor"),
        P("section", "tensor", None),
        P("section", None, "tensor", None, None),
        P("section", None, "tensor", None, None),
        P(),
        P(),
        P(),
        P(),
        P(None, "tensor"),
    )
    return jax.shard_map(
        on_device, mesh=mesh, in_specs=placed, out_specs=P("section", "tensor"), check_vma=False
    )
```

profile of v0, /device:TPU:5, one launch (start us, length us, event | category | flops | bytes accessed | tf_op | source)
XLA Modules:
  0.0 953.8 jit_solution(4745867860651046607)
XLA Ops:
  7.2 939.2 %while.17 = (s32[]{:T(128)}, bf16[8,576]{1,0:T(8,128)(2,1)S(1)}, s32[]{:T(128)}, s32[32]{0:T(128)}, f32[1,4608]{1,0:T(1,128)}, /*index=5*/bf16[4608,512]{1,0:T(8...) while((s32[]{:T(128)}, bf16[8,576]{1,0:T(8,128)(2,1)S(1)}, ...), condition=%wide.region_5.6_spmd.clone, body=%wide.region_0.5_spmd.clone.sunk | while | flops 119565752 | bytes 38957684 | solution.py:156
  7.3 24.9 %all-gather.3 = bf16[8,576,8]{1,2,0:T(8,128)(2,1)S(1)} all-gather(bf16[1,576,8]{1,2,0:T(8,128)(2,1)S(1)} %bitcast.87), channel_id=1, replica_groups=mesh['section'=4,'tensor'=8] {'tensor'}, dimensions={0}, use_global_device_ids=true | all-gather | bytes 82944 | tf_op jit(solution)/shard_map/while/body/eval_jaxpr/all_gather | solution.py:105
  33.3 3.2 convolution_bitcast_fusion.4
  41.2 3.7 convolution_convert_fusion.3
  45.2 73.4 %all-reduce.2.cloned.1.call-done = bf16[8,4608]{1,0:T(8,128)(2,1)} async-done(((bf16[8,4608]{1,0:T(8,128)(2,1)}), bf16[8,4608]{1,0:T(8,128)(2,1)}) %all-reduce.2.cloned.1.call-update) | async-done | bytes 73744 | tf_op jit(solution)/shard_map/while/body/eval_jaxpr/psum | solution.py:140
  124.4 24.6 %all-gather.3 = bf16[8,576,8]{1,2,0:T(8,128)(2,1)S(1)} all-gather(bf16[1,576,8]{1,2,0:T(8,128)(2,1)S(1)} %bitcast.87), channel_id=1, replica_groups=mesh['section'=4,'tensor'=8] {'tensor'}, dimensions={0}, use_global_device_ids=true | all-gather | bytes 82944 | tf_op jit(solution)/shard_map/while/body/eval_jaxpr/all_gather | solution.py:105
  150.2 3.2 convolution_bitcast_fusion.4
  158.1 3.7 convolution_convert_fusion.3
  162.1 74.0 %all-reduce.2.cloned.1.call-done = bf16[8,4608]{1,0:T(8,128)(2,1)} async-done(((bf16[8,4608]{1,0:T(8,128)(2,1)}), bf16[8,4608]{1,0:T(8,128)(2,1)}) %all-reduce.2.cloned.1.call-update) | async-done | bytes 73744 | tf_op jit(solution)/shard_map/while/body/eval_jaxpr/psum | solution.py:140
  241.9 24.6 %all-gather.3 = bf16[8,576,8]{1,2,0:T(8,128)(2,1)S(1)} all-gather(bf16[1,576,8]{1,2,0:T(8,128)(2,1)S(1)} %bitcast.87), channel_id=1, replica_groups=mesh['section'=4,'tensor'=8] {'tensor'}, dimensions={0}, use_global_device_ids=true | all-gather | bytes 82944 | tf_op jit(solution)/shard_map/while/body/eval_jaxpr/all_gather | solution.py:105
  267.6 3.2 convolution_bitcast_fusion.4
  275.5 3.7 convolution_convert_fusion.3
  279.5 74.0 %all-reduce.2.cloned.1.call-done = bf16[8,4608]{1,0:T(8,128)(2,1)} async-done(((bf16[8,4608]{1,0:T(8,128)(2,1)}), bf16[8,4608]{1,0:T(8,128)(2,1)}) %all-reduce.2.cloned.1.call-update) | async-done | bytes 73744 | tf_op jit(solution)/shard_map/while/body/eval_jaxpr/psum | solution.py:140
  359.3 24.6 %all-gather.3 = bf16[8,576,8]{1,2,0:T(8,128)(2,1)S(1)} all-gather(bf16[1,576,8]{1,2,0:T(8,128)(2,1)S(1)} %bitcast.87), channel_id=1, replica_groups=mesh['section'=4,'tensor'=8] {'tensor'}, dimensions={0}, use_global_device_ids=true | all-gather | bytes 82944 | tf_op jit(solution)/shard_map/while/body/eval_jaxpr/all_gather | solution.py:105
  385.0 3.2 convolution_bitcast_fusion.4
  392.9 3.7 convolution_convert_fusion.3
  397.0 74.0 %all-reduce.2.cloned.1.call-done = bf16[8,4608]{1,0:T(8,128)(2,1)} async-done(((bf16[8,4608]{1,0:T(8,128)(2,1)}), bf16[8,4608]{1,0:T(8,128)(2,1)}) %all-reduce.2.cloned.1.call-update) | async-done | bytes 73744 | tf_op jit(solution)/shard_map/while/body/eval_jaxpr/psum | solution.py:140
  476.7 24.6 %all-gather.3 = bf16[8,576,8]{1,2,0:T(8,128)(2,1)S(1)} all-gather(bf16[1,576,8]{1,2,0:T(8,128)(2,1)S(1)} %bitcast.87), channel_id=1, replica_groups=mesh['section'=4,'tensor'=8] {'tensor'}, dimensions={0}, use_global_device_ids=true | all-gather | bytes 82944 | tf_op jit(solution)/shard_map/while/body/eval_jaxpr/all_gather | solution.py:105
  502.5 3.2 convolution_bitcast_fusion.4
  510.3 3.7 convolution_convert_fusion.3
  514.4 74.0 %all-reduce.2.cloned.1.call-done = bf16[8,4608]{1,0:T(8,128)(2,1)} async-done(((bf16[8,4608]{1,0:T(8,128)(2,1)}), bf16[8,4608]{1,0:T(8,128)(2,1)}) %all-reduce.2.cloned.1.call-update) | async-done | bytes 73744 | tf_op jit(solution)/shard_map/while/body/eval_jaxpr/psum | solution.py:140
  594.1 24.6 %all-gather.3 = bf16[8,576,8]{1,2,0:T(8,128)(2,1)S(1)} all-gather(bf16[1,576,8]{1,2,0:T(8,128)(2,1)S(1)} %bitcast.87), channel_id=1, replica_groups=mesh['section'=4,'tensor'=8] {'tensor'}, dimensions={0}, use_global_device_ids=true | all-gather | bytes 82944 | tf_op jit(solution)/shard_map/while/body/eval_jaxpr/all_gather | solution.py:105
  619.9 3.2 convolution_bitcast_fusion.4
  627.8 3.7 convolution_convert_fusion.3
  631.8 74.0 %all-reduce.2.cloned.1.call-done = bf16[8,4608]{1,0:T(8,128)(2,1)} async-done(((bf16[8,4608]{1,0:T(8,128)(2,1)}), bf16[8,4608]{1,0:T(8,128)(2,1)}) %all-reduce.2.cloned.1.call-update) | async-done | bytes 73744 | tf_op jit(solution)/shard_map/while/body/eval_jaxpr/psum | solution.py:140
  711.6 24.6 %all-gather.3 = bf16[8,576,8]{1,2,0:T(8,128)(2,1)S(1)} all-gather(bf16[1,576,8]{1,2,0:T(8,128)(2,1)S(1)} %bitcast.87), channel_id=1, replica_groups=mesh['section'=4,'tensor'=8] {'tensor'}, dimensions={0}, use_global_device_ids=true | all-gather | bytes 82944 | tf_op jit(solution)/shard_map/while/body/eval_jaxpr/all_gather | solution.py:105
  737.3 3.2 convolution_bitcast_fusion.4
  745.2 3.7 convolution_convert_fusion.3
  749.2 74.0 %all-reduce.2.cloned.1.call-done = bf16[8,4608]{1,0:T(8,128)(2,1)} async-done(((bf16[8,4608]{1,0:T(8,128)(2,1)}), bf16[8,4608]{1,0:T(8,128)(2,1)}) %all-reduce.2.cloned.1.call-update) | async-done | bytes 73744 | tf_op jit(solution)/shard_map/while/body/eval_jaxpr/psum | solution.py:140
  829.0 24.6 %all-gather.3 = bf16[8,576,8]{1,2,0:T(8,128)(2,1)S(1)} all-gather(bf16[1,576,8]{1,2,0:T(8,128)(2,1)S(1)} %bitcast.87), channel_id=1, replica_groups=mesh['section'=4,'tensor'=8] {'tensor'}, dimensions={0}, use_global_device_ids=true | all-gather | bytes 82944 | tf_op jit(solution)/shard_map/while/body/eval_jaxpr/all_gather | solution.py:105
  862.6 3.7 convolution_convert_fusion.3
  866.7 74.0 %all-reduce.2.cloned.1.call-done = bf16[8,4608]{1,0:T(8,128)(2,1)} async-done(((bf16[8,4608]{1,0:T(8,128)(2,1)}), bf16[8,4608]{1,0:T(8,128)(2,1)}) %all-reduce.2.cloned.1.call-update) | async-done | bytes 73744 | tf_op jit(solution)/shard_map/while/body/eval_jaxpr/psum | solution.py:140
  (443 shorter events, 98.9 us)
Async XLA Ops:
  7.2 31.6 %copy-start = (bf16[4608,256]{1,0:T(8,128)(2,1)S(1)}, bf16[4608,256]{1,0:T(8,128)(2,1)}, u32[]{:S(2)}) copy-start(bf16[4608,256]{1,0:T(8,128)(2,1)} %get-tuple-element.755) | copy-start | bytes 7077892 | tf_op jit(solution)/shard_map/while
  7.2 111.4 %all-reduce.2.cloned.1.call-start = ((), (), s32[]{:S(2)}) async-start(), calls=%async_computation | async-start | bytes 147456 | tf_op jit(solution)/shard_map/while/body/eval_jaxpr/psum | solution.py:140
  37.3 83.3 %copy-start.6 = (bf16[512,576]{0,1:T(8,128)(2,1)S(1)}, bf16[512,576]{0,1:T(8,128)(2,1)}, u32[]{:S(2)}) copy-start(bf16[512,576]{0,1:T(8,128)(2,1)} %get-tuple-element.764) | copy-start | bytes 1769476 | tf_op jit(solution)/shard_map/while
  120.9 3.5 collective-permute-start
  124.4 31.3 %copy-start = (bf16[4608,256]{1,0:T(8,128)(2,1)S(1)}, bf16[4608,256]{1,0:T(8,128)(2,1)}, u32[]{:S(2)}) copy-start(bf16[4608,256]{1,0:T(8,128)(2,1)} %get-tuple-element.755) | copy-start | bytes 7077892 | tf_op jit(solution)/shard_map/while
  124.4 111.7 %all-reduce.2.cloned.1.call-start = ((), (), s32[]{:S(2)}) async-start(), calls=%async_computation | async-start | bytes 147456 | tf_op jit(solution)/shard_map/while/body/eval_jaxpr/psum | solution.py:140
  154.2 83.9 %copy-start.6 = (bf16[512,576]{0,1:T(8,128)(2,1)S(1)}, bf16[512,576]{0,1:T(8,128)(2,1)}, u32[]{:S(2)}) copy-start(bf16[512,576]{0,1:T(8,128)(2,1)} %get-tuple-element.764) | copy-start | bytes 1769476 | tf_op jit(solution)/shard_map/while
  238.3 3.5 collective-permute-start
  241.8 31.3 %copy-start = (bf16[4608,256]{1,0:T(8,128)(2,1)S(1)}, bf16[4608,256]{1,0:T(8,128)(2,1)}, u32[]{:S(2)}) copy-start(bf16[4608,256]{1,0:T(8,128)(2,1)} %get-tuple-element.755) | copy-start | bytes 7077892 | tf_op jit(solution)/shard_map/while
  241.8 111.7 %all-reduce.2.cloned.1.call-start = ((), (), s32[]{:S(2)}) async-start(), calls=%async_computation | async-start | bytes 147456 | tf_op jit(solution)/shard_map/while/body/eval_jaxpr/psum | solution.py:140
  271.6 83.9 %copy-start.6 = (bf16[512,576]{0,1:T(8,128)(2,1)S(1)}, bf16[512,576]{0,1:T(8,128)(2,1)}, u32[]{:S(2)}) copy-start(bf16[512,576]{0,1:T(8,128)(2,1)} %get-tuple-element.764) | copy-start | bytes 1769476 | tf_op jit(solution)/shard_map/while
  355.7 3.5 collective-permute-start
  359.3 31.3 %copy-start = (bf16[4608,256]{1,0:T(8,128)(2,1)S(1)}, bf16[4608,256]{1,0:T(8,128)(2,1)}, u32[]{:S(2)}) copy-start(bf16[4608,256]{1,0:T(8,128)(2,1)} %get-tuple-element.755) | copy-start | bytes 7077892 | tf_op jit(solution)/shard_map/while
  359.3 111.7 %all-reduce.2.cloned.1.call-start = ((), (), s32[]{:S(2)}) async-start(), calls=%async_computation | async-start | bytes 147456 | tf_op jit(solution)/shard_map/while/body/eval_jaxpr/psum | solution.py:140
  389.0 83.9 %copy-start.6 = (bf16[512,576]{0,1:T(8,128)(2,1)S(1)}, bf16[512,576]{0,1:T(8,128)(2,1)}, u32[]{:S(2)}) copy-start(bf16[512,576]{0,1:T(8,128)(2,1)} %get-tuple-element.764) | copy-start | bytes 1769476 | tf_op jit(solution)/shard_map/while
  473.2 3.5 collective-permute-start
  476.7 31.3 %copy-start = (bf16[4608,256]{1,0:T(8,128)(2,1)S(1)}, bf16[4608,256]{1,0:T(8,128)(2,1)}, u32[]{:S(2)}) copy-start(bf16[4608,256]{1,0:T(8,128)(2,1)} %get-tuple-element.755) | copy-start | bytes 7077892 | tf_op jit(solution)/shard_map/while
  476.7 111.7 %all-reduce.2.cloned.1.call-start = ((), (), s32[]{:S(2)}) async-start(), calls=%async_computation | async-start | bytes 147456 | tf_op jit(solution)/shard_map/while/body/eval_jaxpr/psum | solution.py:140
  506.5 83.9 %copy-start.6 = (bf16[512,576]{0,1:T(8,128)(2,1)S(1)}, bf16[512,576]{0,1:T(8,128)(2,1)}, u32[]{:S(2)}) copy-start(bf16[512,576]{0,1:T(8,128)(2,1)} %get-tuple-element.764) | copy-start | bytes 1769476 | tf_op jit(solution)/shard_map/while
  590.6 3.5 collective-permute-start
  594.1 31.3 %copy-start = (bf16[4608,256]{1,0:T(8,128)(2,1)S(1)}, bf16[4608,256]{1,0:T(8,128)(2,1)}, u32[]{:S(2)}) copy-start(bf16[4608,256]{1,0:T(8,128)(2,1)} %get-tuple-element.755) | copy-start | bytes 7077892 | tf_op jit(solution)/shard_map/while
  594.1 111.7 %all-reduce.2.cloned.1.call-start = ((), (), s32[]{:S(2)}) async-start(), calls=%async_computation | async-start | bytes 147456 | tf_op jit(solution)/shard_map/while/body/eval_jaxpr/psum | solution.py:140
  623.9 83.9 %copy-start.6 = (bf16[512,576]{0,1:T(8,128)(2,1)S(1)}, bf16[512,576]{0,1:T(8,128)(2,1)}, u32[]{:S(2)}) copy-start(bf16[512,576]{0,1:T(8,128)(2,1)} %get-tuple-element.764) | copy-start | bytes 1769476 | tf_op jit(solution)/shard_map/while
  708.0 3.5 collective-permute-start
  711.5 31.3 %copy-start = (bf16[4608,256]{1,0:T(8,128)(2,1)S(1)}, bf16[4608,256]{1,0:T(8,128)(2,1)}, u32[]{:S(2)}) copy-start(bf16[4608,256]{1,0:T(8,128)(2,1)} %get-tuple-element.755) | copy-start | bytes 7077892 | tf_op jit(solution)/shard_map/while
  711.5 111.7 %all-reduce.2.cloned.1.call-start = ((), (), s32[]{:S(2)}) async-start(), calls=%async_computation | async-start | bytes 147456 | tf_op jit(solution)/shard_map/while/body/eval_jaxpr/psum | solution.py:140
  741.3 83.9 %copy-start.6 = (bf16[512,576]{0,1:T(8,128)(2,1)S(1)}, bf16[512,576]{0,1:T(8,128)(2,1)}, u32[]{:S(2)}) copy-start(bf16[512,576]{0,1:T(8,128)(2,1)} %get-tuple-element.764) | copy-start | bytes 1769476 | tf_op jit(solution)/shard_map/while
  825.4 3.5 collective-permute-start
  829.0 31.3 %copy-start = (bf16[4608,256]{1,0:T(8,128)(2,1)S(1)}, bf16[4608,256]{1,0:T(8,128)(2,1)}, u32[]{:S(2)}) copy-start(bf16[4608,256]{1,0:T(8,128)(2,1)} %get-tuple-element.755) | copy-start | bytes 7077892 | tf_op jit(solution)/shard_map/while
  829.0 111.7 %all-reduce.2.cloned.1.call-start = ((), (), s32[]{:S(2)}) async-start(), calls=%async_computation | async-start | bytes 147456 | tf_op jit(solution)/shard_map/while/body/eval_jaxpr/psum | solution.py:140
  858.7 83.9 %copy-start.6 = (bf16[512,576]{0,1:T(8,128)(2,1)S(1)}, bf16[512,576]{0,1:T(8,128)(2,1)}, u32[]{:S(2)}) copy-start(bf16[512,576]{0,1:T(8,128)(2,1)} %get-tuple-element.764) | copy-start | bytes 1769476 | tf_op jit(solution)/shard_map/while
  942.9 3.5 collective-permute-start
  (48 other events, 509.6 us)
Sparse Core Ops, SparseCore 0:
  45.0 73.5 all-reduce.1
  161.9 74.1 all-reduce.1
  279.3 74.1 all-reduce.1
  396.8 74.1 all-reduce.1
  514.2 74.1 all-reduce.1
  631.6 74.1 all-reduce.1
  749.0 74.1 all-reduce.1
  866.5 74.1 all-reduce.1
where the time goes:
time: 959 us; the launch traced here: 954 us
  waiting for transfers between devices  598 us (62%)
  blocking collectives  197 us (21%)
  matrix products  86.4 us (9%)
  other arithmetic  29.1 us (3%)
  starting transfers between devices  21.7 us (2%)
  between operations  13.4 us (1%)
    psum x8, waiting for transfers between devices, advance(): lax.psum(partial_sum.astype(jnp.bfloat16), 'tensor').astype(jnp.float32)  591 us
    all_gather x8, blocking collectives, advance(): features = lax.all_gather(current, 'tensor', axis=1, tiled=True)  197 us
    dot_general x8, matrix products, advance(): jnp.dot(heads_out, out_weight, preferred_element_type=jnp.float32)  29.6 us
    dot_general x8, matrix products, advance(): jnp.dot(normed, query_weight, preferred_element_type=jnp.float32)  25.5 us
    ppermute x8, starting transfers between devices, from_behind(): return lax.ppermute(value, axis, pairs)  21.7 us
  transfers between devices with their start and end apart: 16, of which 16 were waited for; matrix products, arithmetic and copies ran while one was open for 0% of the time, Pallas kernels for 0%

commit v1 on v0

v1 whole, which is shorter than its diff:
```python
import functools
import math

import jax
import jax.numpy as jnp
from jax import lax
from jax.experimental import pallas as pl
from jax.experimental.pallas import tpu as pltpu
from jax.sharding import PartitionSpec as P

MESH = pl.DeviceIdType.MESH
epsilon = 1e-06
softcap_limit = 50.0
BLOCK = 16
f32 = jnp.float32
bf16 = jnp.bfloat16


def kernel(
    S, T,
    lengths, concept, steer_layer, strength,
    resid, pre, post, wq, wk, wv, wo, kc, vc, dirs,
    out_ref,
    wq_v, wk_v, wv_v, wo_v, kc_v, vc_v, dirs_v,
    xg, xprev, x_ref, base, st, dself, gates, lens,
    qs, ks, vs, heads, part, rs, msg, ag, fin_x, fin_p, fin_s, fin_f,
    w_sem, xg_ss, xg_rs, xf_sem, st_ss, st_rs, rs_ss, rs_rs, ag_ss, ag_rs,
    fx_ss, fx_rs, fp_ss, fp_rs, fs_ss, fs_rs,
):
    s = lax.axis_index("section")
    t = lax.axis_index("tensor")
    N = S * T
    R, D = x_ref.shape
    rc, W = resid.shape
    HD = kc_v.shape[-1]
    CTX = kc_v.shape[2]
    KL = kc_v.shape[1]
    H = qs.shape[0]
    group = H // KL
    G = R // BLOCK
    F = T // G
    C = D // F
    per = T // F
    sper = BLOCK // rc
    last = S - 1
    half = HD // 2
    scale = float(D // (H * T)) ** (-0.5)

    def wait(ref, sem):
        pltpu.make_async_copy(ref, ref, sem).wait()

    def remote(src, dst, ss, rsem, ds, dt):
        return pltpu.make_async_remote_copy(
            src_ref=src, dst_ref=dst, send_sem=ss, recv_sem=rsem,
            device_id=(ds, dt), device_id_type=MESH)

    def send(src, dst, ss, rsem, ds, dt):
        mine = (ds == s) & (dt == t)

        @pl.when(mine)
        def _():
            pltpu.make_async_copy(src, dst, rsem).start()

        @pl.when(jnp.logical_not(mine))
        def _():
            remote(src, dst, ss, rsem, ds, dt).start()

    def sent(src, ss, ds, dt):
        @pl.when(jnp.logical_not((ds == s) & (dt == t)))
        def _():
            wait(src, ss)

    loads = [
        pltpu.make_async_copy(a.at[0], b, w_sem.at[i])
        for i, (a, b) in enumerate(
            [(wq, wq_v), (wk, wk_v), (wv, wv_v), (kc, kc_v), (vc, vc_v), (wo, wo_v)])
    ] + [pltpu.make_async_copy(dirs, dirs_v, w_sem.at[6])]
    for one in loads:
        one.start()

    barrier = pltpu.get_barrier_semaphore()
    me = s * T + t

    def greet(n, carry):
        other = lax.rem(me + n, N)
        pl.semaphore_signal(barrier, inc=1, device_id=(other // T, lax.rem(other, T)),
                            device_id_type=MESH)
        return carry

    lax.fori_loop(1, N, greet, 0)
    pl.semaphore_wait(barrier, N - 1)

    for k in range(T):
        dt = lax.rem(t + k, T)
        send(resid, xg.at[s, t], xg_ss.at[k], xg_rs.at[s, t], 0, dt)

    rows = lax.broadcasted_iota(jnp.int32, (R, HD), 0)
    zero_i = jnp.zeros((R, HD), jnp.int32)

    def gather(i, carry):
        a, b, c, d = carry
        hit = rows == i
        return (jnp.where(hit, lengths[i], a), jnp.where(hit, concept[i], b),
                jnp.where(hit, steer_layer[i], c), jnp.where(hit, strength[i], d))

    len_v, con_v, lay_v, str_v = lax.fori_loop(
        0, R, gather, (zero_i, zero_i, zero_i, jnp.zeros((R, HD), f32)))
    lens[...] = len_v
    gates[...] = str_v * (lay_v == last).astype(f32)
    lane = lax.broadcasted_iota(jnp.int32, (R, HD), 1)
    frequency = jnp.exp(lax.rem(lane, half).astype(f32) * (-2.0 * math.log(10000.0) / HD))
    angle = len_v.astype(f32) * frequency
    cosine = jnp.cos(angle)
    sine = jnp.sin(angle)
    sine = jnp.where(lane < half, -sine, sine)

    loads[6].wait()
    nc = dirs_v.shape[0]
    one_hot = (con_v[:, 0:1] == lax.broadcasted_iota(jnp.int32, (R, nc), 1)).astype(f32).astype(bf16)
    picked = jnp.dot(one_hot, dirs_v[...], preferred_element_type=f32)
    dself[...] = picked

    @pl.when(s == 0)
    def _():
        for a in range(S):
            for b in range(T):
                wait(xg.at[a, b], xg_rs.at[a, b])
            base[a * rc:(a + 1) * rc, :] = jnp.concatenate(
                [xg[a, b].astype(f32) for b in range(T)], axis=1)

    @pl.when(s > 0)
    def _():
        st[t] = picked.astype(bf16)
        wait(xprev, xf_sem.at[1])
        for k in range(1, T):
            dt = lax.rem(t + k, T)
            remote(st.at[t], st.at[t], st_ss.at[k], st_rs.at[t], s, dt).start()
        for k in range(1, T):
            b = lax.rem(t + k, T)
            wait(st.at[b], st_rs.at[b])
        gate = (str_v * (lay_v == s - 1).astype(f32))[:, 0:1]
        full = jnp.concatenate([st[b].astype(f32) for b in range(T)], axis=1)
        base[...] = xprev[...].astype(f32) + gate * full
        for o in range(T):
            wait(ag.at[o], ag_rs.at[o])
        for rg in range(G):
            total = jnp.zeros((BLOCK, 1), f32)
            for q in range(F):
                tail = ag[rg * F + q, :, C:C + 128].astype(f32)
                total = total + tail[:, 0:1] + tail[:, 64:65]
            inv = lax.rsqrt(total / D + epsilon)
            for q in range(F):
                place = (slice(rg * BLOCK, (rg + 1) * BLOCK), slice(q * C, (q + 1) * C))
                base[place] = base[place] + inv * ag[rg * F + q, :, 0:C].astype(f32)

    x_bf = base[...].astype(bf16)
    x_ref[...] = x_bf

    my_rg = t // F
    my_q = lax.rem(t, F)
    my_cols = pl.ds(pl.multiple_of(my_q * C, 128), C)
    x_piece = x_ref.at[pl.ds(pl.multiple_of(my_rg * BLOCK, BLOCK), BLOCK), my_cols]
    takers = [(my_rg * sper + a, my_q * per + b, a * per + b)
              for a in range(sper) for b in range(per)]

    @pl.when(s < last)
    def _():
        remote(x_ref, xprev, xf_sem.at[0], xf_sem.at[1], s + 1, t).start()

    @pl.when(s == last)
    def _():
        for ds, dt, n in takers:
            send(x_piece, fin_x, fx_ss.at[n], fx_rs, ds, dt)

    xf = x_bf.astype(f32)
    inv = lax.rsqrt(jnp.mean(xf * xf, axis=1, keepdims=True) + epsilon)
    normed = (xf * inv * pre[...]).astype(bf16)

    def rope(v):
        return (v * cosine + pltpu.roll(v, half, 1) * sine).astype(bf16).astype(f32)

    loads[0].wait()
    q_all = jnp.dot(normed, wq_v[...], preferred_element_type=f32)
    for h in range(H):
        qs[h] = rope(q_all[:, h * HD:(h + 1) * HD])
    loads[1].wait()
    k_all = jnp.dot(normed, wk_v[...], preferred_element_type=f32)
    loads[2].wait()
    v_all = jnp.dot(normed, wv_v[...], preferred_element_type=f32)
    for h in range(KL):
        ks[h] = rope(k_all[:, h * HD:(h + 1) * HD])
        vs[h] = v_all[:, h * HD:(h + 1) * HD].astype(bf16).astype(f32)

    loads[3].wait()
    loads[4].wait()
    span = 8 * CTX
    col = lax.broadcasted_iota(jnp.int32, (8 * group, span), 1)
    row = lax.broadcasted_iota(jnp.int32, (8 * group, span), 0)
    same = (col // CTX) == lax.rem(row, 8)
    spot = lax.rem(col, CTX)
    for i in range(R // 8):
        r0 = 8 * i
        limit = jnp.concatenate([lens[r0:r0 + 8, 0:1]] * group, axis=0)
        valid = same & (spot < limit)
        for h in range(KL):
            qq = jnp.concatenate([qs[h * group + g, r0:r0 + 8, :] for g in range(group)], axis=0)
            kk = jnp.concatenate([ks[h, r0:r0 + 8, :]] * group, axis=0)
            vv = jnp.concatenate([vs[h, r0:r0 + 8, :]] * group, axis=0)
            keys = kc_v[r0:r0 + 8, h].reshape(span, HD)
            values = vc_v[r0:r0 + 8, h].reshape(span, HD)
            scores = lax.dot_general(qq.astype(bf16), keys, (((1,), (1,)), ((), ())),
                                     preferred_element_type=f32) * scale
            own = jnp.sum(qq * kk, axis=1, keepdims=True) * scale
            weight = jnp.where(
                valid,
                jnp.exp(softcap_limit * jnp.tanh(scores / softcap_limit) - softcap_limit), 0.0)
            own_w = jnp.exp(softcap_limit * jnp.tanh(own / softcap_limit) - softcap_limit)
            total = jnp.sum(weight, axis=1, keepdims=True) + own_w
            probs = (weight / total).astype(bf16)
            own_p = (own_w / total).astype(bf16).astype(f32)
            mixed = jnp.dot(probs, values, preferred_element_type=f32) + own_p * vv
            for g in range(group):
                c0 = (h * group + g) * HD
                heads[r0:r0 + 8, c0:c0 + HD] = mixed[8 * g:8 * g + 8, :]

    heads_bf = heads[...].astype(bf16)
    loads[5].wait()
    for q in range(F):
        res = jnp.dot(heads_bf, wo_v[:, q * C:(q + 1) * C],
                      preferred_element_type=f32).astype(bf16)
        for rg in range(G):
            o = rg * F + q
            part[o] = res[rg * BLOCK:(rg + 1) * BLOCK, :]
            send(part.at[o], rs.at[t], rs_ss.at[o], rs_rs.at[t], s, o)

    summed = jnp.zeros((BLOCK, C), f32)
    for o in range(T):
        wait(rs.at[o], rs_rs.at[o])
        summed = summed + rs[o].astype(f32)
    squares = jnp.sum(summed * summed, axis=1, keepdims=True)
    high = squares.astype(bf16).astype(f32)
    msg[:, 0:C] = (summed * post[:, my_cols]).astype(bf16)
    tail_lane = lax.broadcasted_iota(jnp.int32, (BLOCK, 128), 1)
    msg[:, C:C + 128] = jnp.where(tail_lane < 64, high, squares - high).astype(bf16)

    @pl.when(s < last)
    def _():
        for k in range(T):
            dt = lax.rem(t + k, T)
            remote(msg, ag.at[t], ag_ss.at[k], ag_rs.at[t], s + 1, dt).start()

    @pl.when(s == last)
    def _():
        for ds, dt, n in takers:
            send(msg.at[:, pl.ds(0, C)], fin_p, fp_ss.at[n], fp_rs, ds, dt)
        for a in range(sper):
            for b in range(T):
                send(msg.at[:, pl.ds(C, 128)], fin_s.at[my_q], fs_ss.at[a * T + b],
                     fs_rs.at[my_q], my_rg * sper + a, b)

    wait(fin_x, fx_rs)
    wait(fin_p, fp_rs)
    total = jnp.zeros((BLOCK, 1), f32)
    for q in range(F):
        wait(fin_s.at[q], fs_rs.at[q])
        tail = fin_s[q].astype(f32)
        total = total + tail[:, 0:1] + tail[:, 64:65]
    inv = lax.rsqrt(total / D + epsilon)
    fin_f[...] = fin_x[...].astype(f32) + inv * fin_p[...].astype(f32)
    here = fin_f[pl.ds(pl.multiple_of(lax.rem(s, sper) * rc, rc), rc), :]
    within = lax.rem(t, per)
    piece = here[:, 0:W]
    for b in range(1, per):
        piece = jnp.where(within == b, here[:, b * W:(b + 1) * W], piece)
    own_rows = pl.ds(pl.multiple_of(s * rc, rc), rc)
    out_ref[...] = (piece + gates[own_rows, :][:, 0:1] * dself[own_rows, :]).astype(bf16)

    for k in range(T):
        sent(resid, xg_ss.at[k], 0, lax.rem(t + k, T))
    for o in range(T):
        sent(part.at[o], rs_ss.at[o], s, o)

    @pl.when(s > 0)
    def _():
        for k in range(1, T):
            wait(st.at[t], st_ss.at[k])

    @pl.when(s < last)
    def _():
        wait(x_ref, xf_sem.at[0])
        for k in range(T):
            wait(msg, ag_ss.at[k])

    @pl.when(s == last)
    def _():
        for ds, dt, n in takers:
            sent(x_piece, fx_ss.at[n], ds, dt)
            sent(msg.at[:, pl.ds(0, C)], fp_ss.at[n], ds, dt)
        for a in range(sper):
            for b in range(T):
                sent(msg.at[:, pl.ds(C, 128)], fs_ss.at[a * T + b], my_rg * sper + a, b)


def on_device(
    S, T,
    resid, pre_gain, post_gain, w_query, w_key, w_value, w_out, key_cache, value_cache,
    lengths, concept, steer_layer, strength, directions,
):
    rc, W = resid.shape
    R = lengths.shape[0]
    D = pre_gain.shape[1]
    HD = key_cache.shape[-1]
    H = w_query.shape[2] // HD
    KL = key_cache.shape[2]
    G = R // BLOCK
    F = T // G
    C = D // F
    per = T // F
    sper = BLOCK // rc
    dma = pltpu.SemaphoreType.DMA
    vm = pltpu.VMEM
    smem = pl.BlockSpec(memory_space=pltpu.SMEM)
    vmem = pl.BlockSpec(memory_space=pltpu.VMEM)
    hbm = pl.BlockSpec(memory_space=pl.ANY)
    scratch = [
        vm(w_query.shape[1:], bf16), vm(w_key.shape[1:], bf16), vm(w_value.shape[1:], bf16),
        vm(w_out.shape[1:], bf16), vm(key_cache.shape[1:], bf16), vm(value_cache.shape[1:], bf16),
        vm(directions.shape, bf16),
        vm((S, T, rc, W), bf16), vm((R, D), bf16), vm((R, D), bf16), vm((R, D), f32),
        vm((T, R, W), bf16), vm((R, W), f32), vm((R, HD), f32), vm((R, HD), jnp.int32),
        vm((H, R, HD), f32), vm((KL, R, HD), f32), vm((KL, R, HD), f32), vm((R, H * HD), f32),
        vm((T, BLOCK, C), bf16), vm((T, BLOCK, C), bf16), vm((BLOCK, C + 128), bf16),
        vm((T, BLOCK, C + 128), bf16), vm((BLOCK, C), bf16), vm((BLOCK, C), bf16),
        vm((F, BLOCK, 128), bf16), vm((BLOCK, C), f32),
        dma((7,)), dma((T,)), dma((S, T)), dma((2,)), dma((T,)), dma((T,)), dma((T,)), dma((T,)),
        dma((T,)), dma((T,)),
        dma((sper * per,)), dma, dma((sper * per,)), dma, dma((sper * T,)), dma((F,)),
    ]
    return pl.pallas_call(
        functools.partial(kernel, S, T),
        out_shape=jax.ShapeDtypeStruct((rc, W), bf16),
        in_specs=[smem] * 4 + [vmem] * 3 + [hbm] * 7,
        out_specs=vmem,
        scratch_shapes=scratch,
        compiler_params=pltpu.CompilerParams(
            collective_id=0, has_side_effects=True, vmem_limit_bytes=48 * 1024 * 1024),
    )(lengths, concept, steer_layer, strength, resid, pre_gain, post_gain,
      w_query, w_key, w_value, w_out, key_cache, value_cache, directions)


def solution(mesh):
    placed = (
        P("section", "tensor"),
        P("section", None),
        P("section", None),
        P("section", None, "tensor"),
        P("section", None, "tensor"),
        P("section", None, "tensor"),
        P("section", "tensor", None),
        P("section", None, "tensor", None, None),
        P("section", None, "tensor", None, None),
        P(),
        P(),
        P(),
        P(),
        P(None, "tensor"),
    )
    S, T = mesh.shape["section"], mesh.shape["tensor"]
    return jax.shard_map(
        functools.partial(on_device, S, T), mesh=mesh, in_specs=placed,
        out_specs=P("section", "tensor"), check_vma=False,
    )
```

time: 959 us -> 91.1 us (0.09)
  waiting for transfers between devices: 598 us -> 0 us
  blocking collectives: 197 us -> 0 us
  matrix products: 86.4 us -> 0 us
  Pallas kernels: 0 us -> 78.8 us
  other arithmetic: 29.1 us -> 0 us
  starting transfers between devices: 21.7 us -> 0 us
  between operations: 13.4 us -> 0.03 us
    psum x8 -> x0, waiting for transfers between devices: 591 us -> none  [advance(): lax.psum(partial_sum.astype(jnp.bfloat16), 'tensor').astype(jnp.float32)]
    all_gather x8 -> x0, blocking collectives: 197 us -> none  [advance(): features = lax.all_gather(current, 'tensor', axis=1, tiled=True)]
    dot_general x64 -> x0, matrix products: 86.4 us -> none  [the longest x8 29.6 us: advance(): jnp.dot(heads_out, out_weight, preferred_element_type=jnp.float32)]
    pallas_call x0 -> x1, Pallas kernels: none -> 78.8 us  [on_device(): pl.pallas_call(functools.partial(kernel, S, T), out_shape=jax.ShapeDtypeS...]
    ppermute x8 -> x0, starting transfers between devices: 21.7 us -> none  [from_behind(): return lax.ppermute(value, axis, pairs)]
  transfers between devices with their start and end apart: 16 -> 0, of which waited for: 16 -> 0; matrix products, arithmetic and copies ran while one was open for 0% -> 0% of each run, Pallas kernels for 0% -> 0%
where the time goes in v1:
time: 91.1 us; the launch traced here: 89.7 us
  Pallas kernels  78.8 us (86%)
  local copies, waits for them, and re-layouts  10.8 us (12%)
    pallas_call x1, Pallas kernels, on_device(): pl.pallas_call(functools.partial(kernel, S, T), out_shape=jax.ShapeDtypeS...  78.8 us
    unnamed x22, local copies, waits for them, and re-layouts  10.8 us

profile of v1, /device:TPU:5, one launch (start us, length us, event | category | flops | bytes accessed | tf_op | source)
XLA Modules:
  0.0 89.7 jit_solution(16611005395502802870)
XLA Ops:
  0.0 1.4 %copy.15.dirs = bf16[512,576]{1,0:T(8,128)(2,1)S(1)} copy(bf16[512,576]{0,1:T(8,128)(2,1)} %param.27) | data formatting | bytes 1179648 | tf_op args[13]
  1.4 0.0 copy-start
  1.4 1.7 %copy-done = bf16[1,4608,256]{2,1,0:T(8,128)(2,1)S(1)} copy-done((bf16[1,4608,256]{2,1,0:T(8,128)(2,1)S(1)}, bf16[1,4608,256]{2,1,0:T(8,128)(2,1)}, u32[]{:S(2)}) %copy-start) | copy-done | bytes 2359320
  3.0 0.0 copy-start.1
  3.0 1.2 %copy-done.1 = bf16[1,32,2,64,128]{4,3,2,1,0:T(8,128)(2,1)S(1)} copy-done((bf16[1,32,2,64,128]{4,3,2,1,0:T(8,128)(2,1)S(1)}, bf16[1,32,2,64,128]{4,3,2,1,0:T(8,128)(2,1)}, u32[]{:S(2)}) %copy-start.1) | copy-done | bytes 1048600
  4.3 0.0 copy-start.2
  4.3 1.2 %copy-done.2 = bf16[1,32,2,64,128]{4,3,2,1,0:T(8,128)(2,1)S(1)} copy-done((bf16[1,32,2,64,128]{4,3,2,1,0:T(8,128)(2,1)S(1)}, bf16[1,32,2,64,128]{4,3,2,1,0:T(8,128)(2,1)}, u32[]{:S(2)}) %copy-start.2) | copy-done | bytes 1048600
  5.5 0.0 copy-start.3
  5.5 0.7 copy-done.3
  6.2 0.0 copy-start.4
  6.2 0.7 copy-done.4
  6.9 0.0 copy-start.5
  6.9 0.7 copy-done.5
  7.6 0.0 copy-start.6
  7.6 0.7 copy-done.6
  8.3 0.0 copy-start.7
  8.3 0.7 copy-done.7
  8.9 0.0 copy-start.8
  8.9 0.7 copy-done.8
  9.6 0.0 copy-start.9
  9.6 0.7 copy-done.9
  10.3 78.8 %shard_map.136 = bf16[8,576]{1,0:T(8,128)(2,1)S(1)} custom-call(s32[32]{0:T(128)S(1)} %copy-done.6, s32[32]{0:T(128)S(1)} %copy-done.7, s32[32]{0:T(128)S(1)} %copy-done.8, f32[32]{0:T(128)S(1)} %copy-done.9, bf16[8,576]{1,0:T(8,128)(2,1)S(1)} %copy-done.5, f32[1,4608]{1,0:T(1,128)S(1)} %copy-done.3, f32[1,4608]{1,0:T(1,128)S(1)} %copy-done.4, ...), custom_call_target="tpu_custom_call" | custom-call | tf_op jit(solution)/shard_map/pallas_call | solution.py:339
  89.1 0.6 copy.17
Async XLA Ops:
  1.4 1.7 %copy-start = (bf16[1,4608,256]{2,1,0:T(8,128)(2,1)S(1)}, bf16[1,4608,256]{2,1,0:T(8,128)(2,1)}, u32[]{:S(2)}) copy-start(bf16[1,4608,256]{2,1,0:T(8,128)(2,1)} %wk.1) | copy-start | bytes 7077892
  3.0 1.2 %copy-start.1 = (bf16[1,32,2,64,128]{4,3,2,1,0:T(8,128)(2,1)S(1)}, bf16[1,32,2,64,128]{4,3,2,1,0:T(8,128)(2,1)}, u32[]{:S(2)}) copy-start(bf16[1,32,2,64,128]{4,3,2,1,0:T(8,128)(2,1)} %kc.1) | copy-start | bytes 3145732
  4.3 1.2 %copy-start.2 = (bf16[1,32,2,64,128]{4,3,2,1,0:T(8,128)(2,1)S(1)}, bf16[1,32,2,64,128]{4,3,2,1,0:T(8,128)(2,1)}, u32[]{:S(2)}) copy-start(bf16[1,32,2,64,128]{4,3,2,1,0:T(8,128)(2,1)} %vc.1) | copy-start | bytes 3145732
  5.5 0.7 copy-start.3
  6.2 0.7 copy-start.4
  6.9 0.7 copy-start.5
  7.6 0.7 copy-start.6
  8.3 0.7 copy-start.7
  8.9 0.7 copy-start.8
  9.6 0.7 copy-start.9

commit v2 on v1

v2 whole, which is shorter than its diff:
```python
import functools
import math

import jax
import jax.numpy as jnp
from jax import lax
from jax.experimental import pallas as pl
from jax.experimental.pallas import tpu as pltpu
from jax.sharding import PartitionSpec as P

MESH = pl.DeviceIdType.MESH
epsilon = 1e-06
softcap_limit = 50.0
BLOCK = 16
f32 = jnp.float32
bf16 = jnp.bfloat16


def kernel(
    S, T,
    lengths_h, concept_h, steer_h, strength_h,
    resid_h, pre_h, post_h, wq, wk, wv, wo, kc, vc, dirs,
    out_ref,
    lengths, concept, steer_layer, strength, resid, pre, post,
    wq_v, wk_v, wv_v, wo_v, kc_v, vc_v, dirs_v,
    xg, xprev, x_ref, base, st, dself, gates, lens,
    qs, ks, vs, heads, part, rs, msg, ag, fin_x, fin_p, fin_s, fin_f,
    w_sem, xg_ss, xg_rs, xf_ss, xf_rs, st_ss, st_rs, rs_ss, rs_rs, ag_ss, ag_rs,
    fx_ss, fx_rs, fp_ss, fp_rs, fs_ss, fs_rs,
):
    s = lax.axis_index("section")
    t = lax.axis_index("tensor")
    N = S * T
    G, _, D = x_ref.shape
    R = G * BLOCK
    rc, W = resid.shape
    HD = kc_v.shape[-1]
    CTX = kc_v.shape[2]
    KL = kc_v.shape[1]
    H = qs.shape[0]
    group = H // KL
    chunks = D // 128
    Wp = fin_f.shape[1]
    sper = BLOCK // rc
    last = S - 1
    half = HD // 2
    scale = float(D // (H * T)) ** (-0.5)

    def begin(o):
        return (o * chunks) // T * 128

    def window(o):
        return pl.ds(pl.multiple_of(begin(o), 128), Wp)

    def wait(ref, sem):
        pltpu.make_async_copy(ref, ref, sem).wait()

    def remote(src, dst, ss, rsem, ds, dt):
        return pltpu.make_async_remote_copy(
            src_ref=src, dst_ref=dst, send_sem=ss, recv_sem=rsem,
            device_id=(ds, dt), device_id_type=MESH)

    def send(src, dst, ss, rsem, ds, dt):
        mine = (ds == s) & (dt == t)

        @pl.when(mine)
        def _():
            pltpu.make_async_copy(src, dst, rsem).start()

        @pl.when(jnp.logical_not(mine))
        def _():
            remote(src, dst, ss, rsem, ds, dt).start()

    def sent(src, ss, ds, dt):
        @pl.when(jnp.logical_not((ds == s) & (dt == t)))
        def _():
            wait(src, ss)

    barrier = pltpu.get_barrier_semaphore()
    me = s * T + t

    def greet(n, carry):
        other = lax.rem(me + n, N)
        pl.semaphore_signal(barrier, inc=1, device_id=(other // T, lax.rem(other, T)),
                            device_id_type=MESH)
        return carry

    lax.fori_loop(1, N, greet, 0)

    pairs = [(resid_h, resid), (lengths_h, lengths), (concept_h, concept), (steer_h, steer_layer),
             (strength_h, strength), (pre_h, pre), (post_h, post), (dirs, dirs_v),
             (wq.at[0], wq_v), (wk.at[0], wk_v), (wv.at[0], wv_v), (kc.at[0], kc_v),
             (vc.at[0], vc_v), (wo.at[0], wo_v)]
    loads = [pltpu.make_async_copy(a, b, w_sem.at[i]) for i, (a, b) in enumerate(pairs)]
    for one in loads:
        one.start()
    loads[0].wait()
    pl.semaphore_wait(barrier, N - 1)

    for k in range(T):
        dt = lax.rem(t + k, T)
        send(resid, xg.at[s, t], xg_ss.at[k], xg_rs.at[s, t], 0, dt)

    for n in range(1, 7):
        loads[n].wait()
    rows = lax.broadcasted_iota(jnp.int32, (R, HD), 0)
    zero_i = jnp.zeros((R, HD), jnp.int32)

    def gather(i, carry):
        a, b, c, d = carry
        hit = rows == i
        return (jnp.where(hit, lengths[i], a), jnp.where(hit, concept[i], b),
                jnp.where(hit, steer_layer[i], c), jnp.where(hit, strength[i], d))

    len_v, con_v, lay_v, str_v = lax.fori_loop(
        0, R, gather, (zero_i, zero_i, zero_i, jnp.zeros((R, HD), f32)))
    lens[...] = len_v
    gates[...] = str_v * (lay_v == last).astype(f32)
    lane = lax.broadcasted_iota(jnp.int32, (R, HD), 1)
    frequency = jnp.exp(lax.rem(lane, half).astype(f32) * (-2.0 * math.log(10000.0) / HD))
    angle = len_v.astype(f32) * frequency
    cosine = jnp.cos(angle)
    sine = jnp.sin(angle)
    sine = jnp.where(lane < half, -sine, sine)

    loads[7].wait()
    nc = dirs_v.shape[1]
    one_hot = (con_v[:, 0:1] == lax.broadcasted_iota(jnp.int32, (R, nc), 1)).astype(f32).astype(bf16)
    picked = lax.dot_general(one_hot, dirs_v[...], (((1,), (1,)), ((), ())),
                             preferred_element_type=f32)
    dself[...] = picked

    @pl.when(s > 0)
    def _():
        st[t] = picked.astype(bf16)
        for a in range(G):
            wait(xprev.at[a], xf_rs.at[a])
        for k in range(1, T):
            dt = lax.rem(t + k, T)
            remote(st.at[t], st.at[t], st_ss.at[k], st_rs.at[t], s, dt).start()
        for k in range(1, T):
            b = lax.rem(t + k, T)
            wait(st.at[b], st_rs.at[b])
        gate = (str_v * (lay_v == s - 1).astype(f32))[:, 0:1]
        full = jnp.concatenate([st[b].astype(f32) for b in range(T)], axis=1)
        for a in range(G):
            cut = slice(a * BLOCK, (a + 1) * BLOCK)
            base[a] = xprev[a].astype(f32) + gate[cut] * full[cut]

    my_cols = window(t)
    span = 8 * CTX
    tiles = BLOCK // 8
    height = tiles * KL * 8 * group
    col = lax.broadcasted_iota(jnp.int32, (height, span), 1)
    row = lax.broadcasted_iota(jnp.int32, (height, span), 0)
    same = (col // CTX) == lax.rem(row, 8)
    spot = lax.rem(col, CTX)
    tail_lane = lax.broadcasted_iota(jnp.int32, (BLOCK, 128), 1)
    piece_lane = lax.broadcasted_iota(jnp.int32, (BLOCK, Wp), 1)
    fresh = piece_lane < begin(t + 1) - begin(t)

    def rope(v, cut):
        return (v * cosine[cut] + pltpu.roll(v, half, 1) * sine[cut]).astype(bf16).astype(f32)

    def total_of(ref, index):
        total = jnp.zeros((BLOCK, 1), f32)
        for o in range(T):
            tail = index(ref, o).astype(f32)
            total = total + tail[:, 0:1] + tail[:, 64:65]
        return lax.rsqrt(total / D + epsilon)

    def enter(a):
        @pl.when(s == 0)
        def _():
            for n in range(sper):
                owner = a * sper + n
                for b in range(T):
                    wait(xg.at[owner, b], xg_rs.at[owner, b])
                base[a, n * rc:(n + 1) * rc, :] = jnp.concatenate(
                    [xg[owner, b].astype(f32) for b in range(T)], axis=1)

        @pl.when(s > 0)
        def _():
            for o in range(T):
                wait(ag.at[a, o], ag_rs.at[a, o])
            inv = total_of(ag, lambda ref, o: ref[a, o, :, Wp:Wp + 128])
            for o in range(T):
                lo = begin(o)
                size = begin(o + 1) - lo
                base[a, :, lo:lo + size] = (
                    base[a, :, lo:lo + size] + inv * ag[a, o, :, 0:size].astype(f32))

        x_bf = base[a].astype(bf16)
        x_ref[a] = x_bf

        @pl.when(s < last)
        def _():
            remote(x_ref.at[a], xprev.at[a], xf_ss.at[a], xf_rs.at[a], s + 1, t).start()

        @pl.when(s == last)
        def _():
            for n in range(sper):
                send(x_ref.at[a, :, my_cols], fin_x, fx_ss.at[a, n], fx_rs, a * sper + n, t)

        xf = x_bf.astype(f32)
        inv = lax.rsqrt(jnp.mean(xf * xf, axis=1, keepdims=True) + epsilon)
        return (xf * inv * pre[...]).astype(bf16)

    def project(a, normed):
        cut = slice(a * BLOCK, (a + 1) * BLOCK)
        if a == 0:
            loads[8].wait()
        q_all = jnp.dot(normed, wq_v[...], preferred_element_type=f32)
        for h in range(H):
            qs[h] = rope(q_all[:, h * HD:(h + 1) * HD], cut)
        if a == 0:
            loads[9].wait()
            loads[10].wait()
        k_all = jnp.dot(normed, wk_v[...], preferred_element_type=f32)
        v_all = jnp.dot(normed, wv_v[...], preferred_element_type=f32)
        for h in range(KL):
            ks[h] = rope(k_all[:, h * HD:(h + 1) * HD], cut)
            vs[h] = v_all[:, h * HD:(h + 1) * HD].astype(bf16).astype(f32)

    def attend(a):
        if a == 0:
            loads[11].wait()
            loads[12].wait()
        units = [(i, h) for i in range(tiles) for h in range(KL)]
        qq = jnp.concatenate([qs[h * group + g, 8 * i:8 * i + 8, :]
                              for i, h in units for g in range(group)], axis=0)
        kk = jnp.concatenate([ks[h, 8 * i:8 * i + 8, :]
                              for i, h in units for g in range(group)], axis=0)
        vv = jnp.concatenate([vs[h, 8 * i:8 * i + 8, :]
                              for i, h in units for g in range(group)], axis=0)
        r0 = a * BLOCK
        limit = jnp.concatenate([lens[r0 + 8 * i:r0 + 8 * i + 8, 0:1]
                                 for i, h in units for g in range(group)], axis=0)
        qb = qq.astype(bf16)
        step = 8 * group
        scores = jnp.concatenate([
            lax.dot_general(qb[n * step:(n + 1) * step],
                            kc_v[r0 + 8 * i:r0 + 8 * i + 8, h].reshape(span, HD),
                            (((1,), (1,)), ((), ())), preferred_element_type=f32)
            for n, (i, h) in enumerate(units)], axis=0) * scale
        own = jnp.sum(qq * kk, axis=1, keepdims=True) * scale
        weight = jnp.where(
            same & (spot < limit),
            jnp.exp(softcap_limit * jnp.tanh(scores / softcap_limit) - softcap_limit), 0.0)
        own_w = jnp.exp(softcap_limit * jnp.tanh(own / softcap_limit) - softcap_limit)
        total = jnp.sum(weight, axis=1, keepdims=True) + own_w
        probs = (weight / total).astype(bf16)
        own_p = (own_w / total).astype(bf16).astype(f32)
        mixed = jnp.concatenate([
            jnp.dot(probs[n * step:(n + 1) * step],
                    vc_v[r0 + 8 * i:r0 + 8 * i + 8, h].reshape(span, HD),
                    preferred_element_type=f32)
            for n, (i, h) in enumerate(units)], axis=0) + own_p * vv
        for n, (i, h) in enumerate(units):
            for g in range(group):
                c0 = (h * group + g) * HD
                heads[8 * i:8 * i + 8, c0:c0 + HD] = mixed[n * step + 8 * g:n * step + 8 * g + 8, :]

    def leave(a):
        if a == 0:
            loads[13].wait()
        part[a] = jnp.dot(heads[...].astype(bf16), wo_v[...],
                          preferred_element_type=f32).astype(bf16)
        for k in range(1, T):
            dt = lax.rem(t + k, T)
            remote(part.at[a, :, window(dt)], rs.at[a, t], rs_ss.at[a, k], rs_rs.at[a, t],
                   s, dt).start()
        rs[a, t] = part[a, :, my_cols]

    def reduce(a):
        for k in range(1, T):
            o = lax.rem(t + k, T)
            wait(rs.at[a, o], rs_rs.at[a, o])
        summed = jnp.zeros((BLOCK, Wp), f32)
        for o in range(T):
            summed = summed + rs[a, o].astype(f32)
        squares = jnp.sum(jnp.where(fresh, summed * summed, 0.0), axis=1, keepdims=True)
        high = squares.astype(bf16).astype(f32)
        msg[a, :, 0:Wp] = (summed * post[:, my_cols]).astype(bf16)
        msg[a, :, Wp:Wp + 128] = jnp.where(tail_lane < 64, high, squares - high).astype(bf16)

        @pl.when(s < last)
        def _():
            for k in range(T):
                dt = lax.rem(t + k, T)
                remote(msg.at[a], ag.at[a, t], ag_ss.at[a, k], ag_rs.at[a, t], s + 1, dt).start()

        @pl.when(s == last)
        def _():
            for n in range(sper):
                ds = a * sper + n
                send(msg.at[a, :, pl.ds(0, Wp)], fin_p, fp_ss.at[a, n], fp_rs, ds, t)
                for b in range(T):
                    send(msg.at[a, :, pl.ds(Wp, 128)], fin_s.at[t], fs_ss.at[a, n * T + b],
                         fs_rs.at[t], ds, b)

    for a in range(G):
        project(a, enter(a))
        if a > 0:
            reduce(a - 1)
        attend(a)
        leave(a)
    reduce(G - 1)

    wait(fin_x, fx_rs)
    wait(fin_p, fp_rs)
    for o in range(T):
        wait(fin_s.at[o], fs_rs.at[o])
    inv = total_of(fin_s, lambda ref, o: ref[o])
    fin_f[...] = fin_x[...].astype(f32) + inv * fin_p[...].astype(f32)
    here = fin_f[pl.ds(pl.multiple_of(lax.rem(s, sper) * rc, rc), rc), :]
    shift = t * W - begin(t)
    piece = here[:, 0:W]
    for b in sorted({(p * W) % 128 for p in range(T)} - {0}):
        piece = jnp.where(shift == b, here[:, b:b + W], piece)
    own_rows = pl.ds(pl.multiple_of(s * rc, rc), rc)
    out_ref[...] = (piece + gates[own_rows, :][:, 0:1] * dself[own_rows, :]).astype(bf16)

    for k in range(T):
        sent(resid, xg_ss.at[k], 0, lax.rem(t + k, T))
    for a in range(G):
        for k in range(1, T):
            wait(part.at[a, :, window(lax.rem(t + k, T))], rs_ss.at[a, k])

    @pl.when(s > 0)
    def _():
        for k in range(1, T):
            wait(st.at[t], st_ss.at[k])

    @pl.when(s < last)
    def _():
        for a in range(G):
            wait(x_ref.at[a], xf_ss.at[a])
            for k in range(T):
                wait(msg.at[a], ag_ss.at[a, k])

    @pl.when(s == last)
    def _():
        for a in range(G):
            for n in range(sper):
                ds = a * sper + n
                sent(x_ref.at[a, :, my_cols], fx_ss.at[a, n], ds, t)
                sent(msg.at[a, :, pl.ds(0, Wp)], fp_ss.at[a, n], ds, t)
                for b in range(T):
                    sent(msg.at[a, :, pl.ds(Wp, 128)], fs_ss.at[a, n * T + b], ds, b)


def on_device(
    S, T,
    resid, pre_gain, post_gain, w_query, w_key, w_value, w_out, key_cache, value_cache,
    lengths, concept, steer_layer, strength, directions,
):
    rc, W = resid.shape
    R = lengths.shape[0]
    D = pre_gain.shape[1]
    HD = key_cache.shape[-1]
    H = w_query.shape[2] // HD
    KL = key_cache.shape[2]
    G = R // BLOCK
    Wp = -(-(D // 128) // T) * 128
    sper = BLOCK // rc
    dma = pltpu.SemaphoreType.DMA
    vm = pltpu.VMEM
    hbm = pl.BlockSpec(memory_space=pltpu.HBM)
    turned = directions.T
    scratch = [
        pltpu.SMEM((R,), jnp.int32), pltpu.SMEM((R,), jnp.int32), pltpu.SMEM((R,), jnp.int32),
        pltpu.SMEM((R,), f32), vm((rc, W), bf16), vm((1, D), f32), vm((1, D), f32),
        vm(w_query.shape[1:], bf16), vm(w_key.shape[1:], bf16), vm(w_value.shape[1:], bf16),
        vm(w_out.shape[1:], bf16), vm(key_cache.shape[1:], bf16), vm(value_cache.shape[1:], bf16),
        vm(turned.shape, bf16),
        vm((S, T, rc, W), bf16), vm((G, BLOCK, D), bf16), vm((G, BLOCK, D), bf16),
        vm((G, BLOCK, D), f32),
        vm((T, R, W), bf16), vm((R, W), f32), vm((R, HD), f32), vm((R, HD), jnp.int32),
        vm((H, BLOCK, HD), f32), vm((KL, BLOCK, HD), f32), vm((KL, BLOCK, HD), f32),
        vm((BLOCK, H * HD), f32),
        vm((G, BLOCK, D), bf16), vm((G, T, BLOCK, Wp), bf16), vm((G, BLOCK, Wp + 128), bf16),
        vm((G, T, BLOCK, Wp + 128), bf16), vm((BLOCK, Wp), bf16), vm((BLOCK, Wp), bf16),
        vm((T, BLOCK, 128), bf16), vm((BLOCK, Wp), f32),
        dma((14,)), dma((T,)), dma((S, T)), dma((G,)), dma((G,)), dma((T,)), dma((T,)),
        dma((G, T)), dma((G, T)), dma((G, T)), dma((G, T)),
        dma((G, sper)), dma, dma((G, sper)), dma, dma((G, sper * T)), dma((T,)),
    ]
    return pl.pallas_call(
        functools.partial(kernel, S, T),
        out_shape=jax.ShapeDtypeStruct((rc, W), bf16),
        in_specs=[hbm] * 14,
        out_specs=pl.BlockSpec(memory_space=pltpu.VMEM),
        scratch_shapes=scratch,
        compiler_params=pltpu.CompilerParams(
            collective_id=0, has_side_effects=True, vmem_limit_bytes=63 * 1024 * 1024),
    )(lengths, concept, steer_layer, strength, resid, pre_gain, post_gain,
      w_query, w_key, w_value, w_out, key_cache, value_cache, turned)


def solution(mesh):
    placed = (
        P("section", "tensor"),
        P("section", None),
        P("section", None),
        P("section", None, "tensor"),
        P("section", None, "tensor"),
        P("section", None, "tensor"),
        P("section", "tensor", None),
        P("section", None, "tensor", None, None),
        P("section", None, "tensor", None, None),
        P(),
        P(),
        P(),
        P(),
        P(None, "tensor"),
    )
    S, T = mesh.shape["section"], mesh.shape["tensor"]
    return jax.shard_map(
        functools.partial(on_device, S, T), mesh=mesh, in_specs=placed,
        out_specs=P("section", "tensor"), check_vma=False,
    )
```

time: 91.1 us -> 78.2 us (0.86); the launches traced: 89.7 us -> 77.9 us
  local copies, waits for them, and re-layouts: 10.8 us -> 1.3 us
  Pallas kernels: 78.8 us -> 76.6 us
    unnamed x22 -> x1, local copies, waits for them, and re-layouts: 10.8 us -> 1.3 us
    pallas_call x1, Pallas kernels: 78.8 us -> 76.6 us  [on_device(): pl.pallas_call(functools.partial(kernel, S, T), out_shape=jax.ShapeDtypeS...]
where the time goes in v2:
time: 78.2 us; the launch traced here: 77.9 us
  Pallas kernels  76.6 us (98%)
  local copies, waits for them, and re-layouts  1.3 us (2%)
    pallas_call x1, Pallas kernels, on_device(): pl.pallas_call(functools.partial(kernel, S, T), out_shape=jax.ShapeDtypeS...  76.6 us

profile of v2, /device:TPU:5, one launch (start us, length us, event | category | flops | bytes accessed | tf_op | source)
XLA Modules:
  0.0 77.9 jit_solution(1888321572970116787)
XLA Ops:
  0.0 76.6 %shard_map.136 = bf16[8,576]{1,0:T(8,128)(2,1)} custom-call(s32[32]{0:T(128)} %lengths_h.1, s32[32]{0:T(128)} %concept_h.1, s32[32]{0:T(128)} %steer_h.1, f32[32]{0:T(128)} %strength_h.1, bf16[8,576]{1,0:T(8,128)(2,1)} %resid_h.1, f32[1,4608]{1,0:T(1,128)} %pre_h.1, f32[1,4608]{1,0:T(1,128)} %post_h.1, bf16[1,4608,512]{2,1,0:T(8,128)(2,1)} %wq.1, ...), custom_call_target="tpu_custom_call" | custom-call | tf_op jit(solution)/shard_map/pallas_call | solution.py:389
  76.6 1.3 %copy.16 = bf16[8,576]{1,0:T(8,128)(2,1)} copy(bf16[8,576]{1,0:T(8,128)(2,1)} %shard_map.136) | data formatting | bytes 18432

commit v3 on v2

--- a/solution.py
+++ b/solution.py
@@ -24,7 +24,7 @@
     lengths, concept, steer_layer, strength, resid, pre, post,
     wq_v, wk_v, wv_v, wo_v, kc_v, vc_v, dirs_v,
     xg, xprev, x_ref, base, st, dself, gates, lens,
-    qs, ks, vs, heads, part, rs, msg, ag, fin_x, fin_p, fin_s, fin_f,
+    proj, qs, ks, vs, heads, part, rs, msg, ag, fin_x, fin_p, fin_s, fin_f,
     w_sem, xg_ss, xg_rs, xf_ss, xf_rs, st_ss, st_rs, rs_ss, rs_rs, ag_ss, ag_rs,
     fx_ss, fx_rs, fp_ss, fp_rs, fs_ss, fs_rs,
 ):
@@ -42,6 +42,10 @@
     chunks = D // 128
     Wp = fin_f.shape[1]
     sper = BLOCK // rc
+    per = next(n for n in range(1, T + 1) if (chunks * n) % T == 0)
+    quarters = T // per
+    GW = chunks * per // T * 128
+    my_j = t // per
     last = S - 1
     half = HD // 2
     scale = float(D // (H * T)) ** (-0.5)
@@ -130,11 +134,28 @@
                              preferred_element_type=f32)
     dself[...] = picked
 
+    def matmul(v, part_rows):
+        return jnp.concatenate([
+            jnp.dot(v, w[part_rows, :], preferred_element_type=f32)
+            for w in (wq_v, wk_v, wv_v)], axis=1)
+
+    @pl.when(s == 0)
+    def _():
+        for a in range(G):
+            for n in range(sper):
+                owner = a * sper + n
+                for b in range(T):
+                    wait(xg.at[owner, b], xg_rs.at[owner, b])
+                base[a, n * rc:(n + 1) * rc, :] = jnp.concatenate(
+                    [xg[owner, b].astype(f32) for b in range(T)], axis=1)
+            x_ref[a] = base[a].astype(bf16)
+            remote(x_ref.at[a], xprev.at[a], xf_ss.at[a], xf_rs.at[a], s + 1, t).start()
+
     @pl.when(s > 0)
     def _():
         st[t] = picked.astype(bf16)
-        for a in range(G):
-            wait(xprev.at[a], xf_rs.at[a])
+        for k in range(T):
+            wait(resid, xg_ss.at[k])
         for k in range(1, T):
             dt = lax.rem(t + k, T)
             remote(st.at[t], st.at[t], st_ss.at[k], st_rs.at[t], s, dt).start()
@@ -145,7 +166,14 @@
         full = jnp.concatenate([st[b].astype(f32) for b in range(T)], axis=1)
         for a in range(G):
             cut = slice(a * BLOCK, (a + 1) * BLOCK)
+            wait(xprev.at[a], xf_rs.at[a])
             base[a] = xprev[a].astype(f32) + gate[cut] * full[cut]
+
+    for n in (8, 9, 10):
+        loads[n].wait()
+    proj[...] = matmul(
+        jnp.concatenate([(base[a] * pre[...]).astype(bf16) for a in range(G)], axis=0),
+        slice(0, D))
 
     my_cols = window(t)
     span = 8 * CTX
@@ -170,30 +198,31 @@
         return lax.rsqrt(total / D + epsilon)
 
     def enter(a):
-        @pl.when(s == 0)
-        def _():
-            for n in range(sper):
-                owner = a * sper + n
-                for b in range(T):
-                    wait(xg.at[owner, b], xg_rs.at[owner, b])
-                base[a, n * rc:(n + 1) * rc, :] = jnp.concatenate(
-                    [xg[owner, b].astype(f32) for b in range(T)], axis=1)
+        cut = slice(a * BLOCK, (a + 1) * BLOCK)
 
         @pl.when(s > 0)
         def _():
-            for o in range(T):
-                wait(ag.at[a, o], ag_rs.at[a, o])
+            acc = None
+            for i in range(quarters):
+                j = lax.rem(my_j + i, quarters)
+                for n in range(per):
+                    wait(ag.at[a, j * per + n], ag_rs.at[a, j * per + n])
+                p = jnp.concatenate(
+                    [ag[a, j * per + n, :, 0:begin(n + 1) - begin(n)].astype(f32)
+                     for n in range(per)], axis=1)
+                at = pl.ds(pl.multiple_of(j * GW, 128), GW)
+                term = matmul((p * pre[:, at]).astype(bf16), at)
+                acc = term if acc is None else acc + term
             inv = total_of(ag, lambda ref, o: ref[a, o, :, Wp:Wp + 128])
             for o in range(T):
                 lo = begin(o)
                 size = begin(o + 1) - lo
                 base[a, :, lo:lo + size] = (
                     base[a, :, lo:lo + size] + inv * ag[a, o, :, 0:size].astype(f32))
-
-        x_bf = base[a].astype(bf16)
-        x_ref[a] = x_bf
-
-        @pl.when(s < last)
+            x_ref[a] = base[a].astype(bf16)
+            proj[cut, :] = proj[cut, :] + inv * acc
+
+        @pl.when((s > 0) & (s < last))
         def _():
             remote(x_ref.at[a], xprev.at[a], xf_ss.at[a], xf_rs.at[a], s + 1, t).start()
 
@@ -202,25 +231,16 @@
             for n in range(sper):
                 send(x_ref.at[a, :, my_cols], fin_x, fx_ss.at[a, n], fx_rs, a * sper + n, t)
 
-        xf = x_bf.astype(f32)
+        xf = x_ref[a].astype(f32)
         inv = lax.rsqrt(jnp.mean(xf * xf, axis=1, keepdims=True) + epsilon)
-        return (xf * inv * pre[...]).astype(bf16)
-
-    def project(a, normed):
-        cut = slice(a * BLOCK, (a + 1) * BLOCK)
-        if a == 0:
-            loads[8].wait()
-        q_all = jnp.dot(normed, wq_v[...], preferred_element_type=f32)
+        all_ = proj[cut, :] * inv
         for h in range(H):
-            qs[h] = rope(q_all[:, h * HD:(h + 1) * HD], cut)
-        if a == 0:
-            loads[9].wait()
-            loads[10].wait()
-        k_all = jnp.dot(normed, wk_v[...], preferred_element_type=f32)
-        v_all = jnp.dot(normed, wv_v[...], preferred_element_type=f32)
+            qs[h] = rope(all_[:, h * HD:(h + 1) * HD], cut)
         for h in range(KL):
-            ks[h] = rope(k_all[:, h * HD:(h + 1) * HD], cut)
-            vs[h] = v_all[:, h * HD:(h + 1) * HD].astype(bf16).astype(f32)
+            c0 = (H + h) * HD
+            ks[h] = rope(all_[:, c0:c0 + HD], cut)
+            c0 = (H + KL + h) * HD
+            vs[h] = all_[:, c0:c0 + HD].astype(bf16).astype(f32)
 
     def attend(a):
         if a == 0:
@@ -261,15 +281,27 @@
                 c0 = (h * group + g) * HD
                 heads[8 * i:8 * i + 8, c0:c0 + HD] = mixed[n * step + 8 * g:n * step + 8 * g + 8, :]
 
+    def targets():
+        k = 0
+        for i in list(range(1, quarters)) + [0]:
+            j = lax.rem(my_j + i, quarters)
+            outs = []
+            for n in range(per if i else per - 1):
+                k += 1
+                inner = n if i else lax.rem(lax.rem(t, per) + n + 1, per)
+                outs.append((j * per + inner, k))
+            yield j, outs
+
     def leave(a):
         if a == 0:
             loads[13].wait()
-        part[a] = jnp.dot(heads[...].astype(bf16), wo_v[...],
-                          preferred_element_type=f32).astype(bf16)
-        for k in range(1, T):
-            dt = lax.rem(t + k, T)
-            remote(part.at[a, :, window(dt)], rs.at[a, t], rs_ss.at[a, k], rs_rs.at[a, t],
-                   s, dt).start()
+        hb = heads[...].astype(bf16)
+        for j, outs in targets():
+            at = pl.ds(pl.multiple_of(j * GW, 128), GW)
+            part[a, :, at] = jnp.dot(hb, wo_v[:, at], preferred_element_type=f32).astype(bf16)
+            for o, k in outs:
+                remote(part.at[a, :, window(o)], rs.at[a, t], rs_ss.at[a, k], rs_rs.at[a, t],
+                       s, o).start()
         rs[a, t] = part[a, :, my_cols]
 
     def reduce(a):
@@ -300,7 +332,7 @@
                          fs_rs.at[t], ds, b)
 
     for a in range(G):
-        project(a, enter(a))
+        enter(a)
         if a > 0:
             reduce(a - 1)
         attend(a)
@@ -321,11 +353,15 @@
     own_rows = pl.ds(pl.multiple_of(s * rc, rc), rc)
     out_ref[...] = (piece + gates[own_rows, :][:, 0:1] * dself[own_rows, :]).astype(bf16)
 
-    for k in range(T):
-        sent(resid, xg_ss.at[k], 0, lax.rem(t + k, T))
+    @pl.when(s == 0)
+    def _():
+        for k in range(1, T):
+            wait(resid, xg_ss.at[k])
+
     for a in range(G):
-        for k in range(1, T):
-            wait(part.at[a, :, window(lax.rem(t + k, T))], rs_ss.at[a, k])
+        for j, outs in targets():
+            for o, k in outs:
+                wait(part.at[a, :, window(o)], rs_ss.at[a, k])
 
     @pl.when(s > 0)
     def _():
@@ -377,6 +413,7 @@
         vm((S, T, rc, W), bf16), vm((G, BLOCK, D), bf16), vm((G, BLOCK, D), bf16),
         vm((G, BLOCK, D), f32),
         vm((T, R, W), bf16), vm((R, W), f32), vm((R, HD), f32), vm((R, HD), jnp.int32),
+        vm((R, (H + 2 * KL) * HD), f32),
         vm((H, BLOCK, HD), f32), vm((KL, BLOCK, HD), f32), vm((KL, BLOCK, HD), f32),
         vm((BLOCK, H * HD), f32),
         vm((G, BLOCK, D), bf16), vm((G, T, BLOCK, Wp), bf16), vm((G, BLOCK, Wp + 128), bf16),

time: 78.2 us -> 73.6 us (0.941)
  Pallas kernels: 76.6 us -> 72 us
    pallas_call x1, Pallas kernels: 76.6 us -> 72 us  [on_device(): pl.pallas_call(functools.partial(kernel, S, T), out_shape=jax.ShapeDtypeS...]
where the time goes in v3:
time: 73.6 us; the launch traced here: 73.3 us
  Pallas kernels  72 us (98%)
  local copies, waits for them, and re-layouts  1.3 us (2%)
    pallas_call x1, Pallas kernels, on_device(): pl.pallas_call(functools.partial(kernel, S, T), out_shape=jax.ShapeDtypeS...  72 us

profile of v3, /device:TPU:5, one launch (start us, length us, event | category | flops | bytes accessed | tf_op | source)
XLA Modules:
  0.0 73.3 jit_solution(7120235851105858402)
XLA Ops:
  0.0 72.0 %shard_map.136 = bf16[8,576]{1,0:T(8,128)(2,1)} custom-call(s32[32]{0:T(128)} %lengths_h.1, s32[32]{0:T(128)} %concept_h.1, s32[32]{0:T(128)} %steer_h.1, f32[32]{0:T(128)} %strength_h.1, bf16[8,576]{1,0:T(8,128)(2,1)} %resid_h.1, f32[1,4608]{1,0:T(1,128)} %pre_h.1, f32[1,4608]{1,0:T(1,128)} %post_h.1, bf16[1,4608,512]{2,1,0:T(8,128)(2,1)} %wq.1, ...), custom_call_target="tpu_custom_call" | custom-call | tf_op jit(solution)/shard_map/pallas_call | solution.py:426
  72.0 1.3 %copy.16 = bf16[8,576]{1,0:T(8,128)(2,1)} copy(bf16[8,576]{1,0:T(8,128)(2,1)} %shard_map.136) | data formatting | bytes 18432

commit v4 on v3

--- a/solution.py
+++ b/solution.py
@@ -11,7 +11,7 @@
 MESH = pl.DeviceIdType.MESH
 epsilon = 1e-06
 softcap_limit = 50.0
-BLOCK = 16
+BLOCK = 32
 f32 = jnp.float32
 bf16 = jnp.bfloat16
 

time: 73.6 us -> 74.8 us (1.016); the launches traced: 73.3 us -> 73.7 us
  no operation moved by 1% of the time
where the time goes in v4:
time: 74.8 us; the launch traced here: 73.7 us
  Pallas kernels  72.4 us (97%)
  local copies, waits for them, and re-layouts  1.3 us (2%)
    pallas_call x1, Pallas kernels, on_device(): pl.pallas_call(functools.partial(kernel, S, T), out_shape=jax.ShapeDtypeS...  72.4 us

profile of v4, /device:TPU:5, one launch (start us, length us, event | category | flops | bytes accessed | tf_op | source)
XLA Modules:
  0.0 73.7 jit_solution(10428660717142032582)
XLA Ops:
  0.0 72.4 %shard_map.136 = bf16[8,576]{1,0:T(8,128)(2,1)} custom-call(s32[32]{0:T(128)} %lengths_h.1, s32[32]{0:T(128)} %concept_h.1, s32[32]{0:T(128)} %steer_h.1, f32[32]{0:T(128)} %strength_h.1, bf16[8,576]{1,0:T(8,128)(2,1)} %resid_h.1, f32[1,4608]{1,0:T(1,128)} %pre_h.1, f32[1,4608]{1,0:T(1,128)} %post_h.1, bf16[1,4608,512]{2,1,0:T(8,128)(2,1)} %wq.1, ...), custom_call_target="tpu_custom_call" | custom-call | tf_op jit(solution)/shard_map/pallas_call | solution.py:426
  72.4 1.3 %copy.16 = bf16[8,576]{1,0:T(8,128)(2,1)} copy(bf16[8,576]{1,0:T(8,128)(2,1)} %shard_map.136) | data formatting | bytes 18432

commit v5 on v3

--- a/solution.py
+++ b/solution.py
@@ -45,7 +45,6 @@
     per = next(n for n in range(1, T + 1) if (chunks * n) % T == 0)
     quarters = T // per
     GW = chunks * per // T * 128
-    my_j = t // per
     last = S - 1
     half = HD // 2
     scale = float(D // (H * T)) ** (-0.5)
@@ -176,6 +175,14 @@
         slice(0, D))
 
     my_cols = window(t)
+    first = T // quarters
+    is_owner = (t >= first) & (t < first + quarters)
+    my_j = jnp.clip(t - first, 0, quarters - 1)
+    my_quarter = pl.ds(pl.multiple_of(my_j * GW, 128), GW)
+
+    def inside(n):
+        return pl.ds(begin(n), Wp)
+
     span = 8 * CTX
     tiles = BLOCK // 8
     height = tiles * KL * 8 * group
@@ -184,15 +191,13 @@
     same = (col // CTX) == lax.rem(row, 8)
     spot = lax.rem(col, CTX)
     tail_lane = lax.broadcasted_iota(jnp.int32, (BLOCK, 128), 1)
-    piece_lane = lax.broadcasted_iota(jnp.int32, (BLOCK, Wp), 1)
-    fresh = piece_lane < begin(t + 1) - begin(t)
 
     def rope(v, cut):
         return (v * cosine[cut] + pltpu.roll(v, half, 1) * sine[cut]).astype(bf16).astype(f32)
 
     def total_of(ref, index):
         total = jnp.zeros((BLOCK, 1), f32)
-        for o in range(T):
+        for o in range(quarters):
             tail = index(ref, o).astype(f32)
             total = total + tail[:, 0:1] + tail[:, 64:65]
         return lax.rsqrt(total / D + epsilon)
@@ -203,22 +208,16 @@
         @pl.when(s > 0)
         def _():
             acc = None
-            for i in range(quarters):
-                j = lax.rem(my_j + i, quarters)
-                for n in range(per):
-                    wait(ag.at[a, j * per + n], ag_rs.at[a, j * per + n])
-                p = jnp.concatenate(
-                    [ag[a, j * per + n, :, 0:begin(n + 1) - begin(n)].astype(f32)
-                     for n in range(per)], axis=1)
-                at = pl.ds(pl.multiple_of(j * GW, 128), GW)
+            for j in range(quarters):
+                wait(ag.at[a, j], ag_rs.at[a, j])
+                at = slice(j * GW, (j + 1) * GW)
+                p = ag[a, j, :, 0:GW].astype(f32)
                 term = matmul((p * pre[:, at]).astype(bf16), at)
                 acc = term if acc is None else acc + term
-            inv = total_of(ag, lambda ref, o: ref[a, o, :, Wp:Wp + 128])
-            for o in range(T):
-                lo = begin(o)
-                size = begin(o + 1) - lo
-                base[a, :, lo:lo + size] = (
-                    base[a, :, lo:lo + size] + inv * ag[a, o, :, 0:size].astype(f32))
+            inv = total_of(ag, lambda ref, o: ref[a, o, :, GW:GW + 128])
+            for j in range(quarters):
+                at = slice(j * GW, (j + 1) * GW)
+                base[a, :, at] = base[a, :, at] + inv * ag[a, j, :, 0:GW].astype(f32)
             x_ref[a] = base[a].astype(bf16)
             proj[cut, :] = proj[cut, :] + inv * acc
 
@@ -281,55 +280,44 @@
                 c0 = (h * group + g) * HD
                 heads[8 * i:8 * i + 8, c0:c0 + HD] = mixed[n * step + 8 * g:n * step + 8 * g + 8, :]
 
-    def targets():
-        k = 0
-        for i in list(range(1, quarters)) + [0]:
-            j = lax.rem(my_j + i, quarters)
-            outs = []
-            for n in range(per if i else per - 1):
-                k += 1
-                inner = n if i else lax.rem(lax.rem(t, per) + n + 1, per)
-                outs.append((j * per + inner, k))
-            yield j, outs
-
     def leave(a):
         if a == 0:
             loads[13].wait()
         hb = heads[...].astype(bf16)
-        for j, outs in targets():
-            at = pl.ds(pl.multiple_of(j * GW, 128), GW)
-            part[a, :, at] = jnp.dot(hb, wo_v[:, at], preferred_element_type=f32).astype(bf16)
-            for o, k in outs:
-                remote(part.at[a, :, window(o)], rs.at[a, t], rs_ss.at[a, k], rs_rs.at[a, t],
-                       s, o).start()
-        rs[a, t] = part[a, :, my_cols]
+        for j in range(quarters):
+            at = slice(j * GW, (j + 1) * GW)
+            part[a, j] = jnp.dot(hb, wo_v[:, at], preferred_element_type=f32).astype(bf16)
+            send(part.at[a, j], rs.at[a, t], rs_ss.at[a, j], rs_rs.at[a, t], s, first + j)
 
     def reduce(a):
-        for k in range(1, T):
-            o = lax.rem(t + k, T)
-            wait(rs.at[a, o], rs_rs.at[a, o])
-        summed = jnp.zeros((BLOCK, Wp), f32)
-        for o in range(T):
-            summed = summed + rs[a, o].astype(f32)
-        squares = jnp.sum(jnp.where(fresh, summed * summed, 0.0), axis=1, keepdims=True)
-        high = squares.astype(bf16).astype(f32)
-        msg[a, :, 0:Wp] = (summed * post[:, my_cols]).astype(bf16)
-        msg[a, :, Wp:Wp + 128] = jnp.where(tail_lane < 64, high, squares - high).astype(bf16)
-
-        @pl.when(s < last)
+        @pl.when(is_owner)
+        def _():
+            summed = jnp.zeros((BLOCK, GW), f32)
+            for o in range(T):
+                wait(rs.at[a, o], rs_rs.at[a, o])
+                summed = summed + rs[a, o].astype(f32)
+            squares = jnp.sum(summed * summed, axis=1, keepdims=True)
+            high = squares.astype(bf16).astype(f32)
+            msg[a, :, 0:GW] = (summed * post[:, my_quarter]).astype(bf16)
+            msg[a, :, GW:GW + 128] = jnp.where(tail_lane < 64, high, squares - high).astype(bf16)
+
+        @pl.when(is_owner & (s < last))
         def _():
             for k in range(T):
                 dt = lax.rem(t + k, T)
-                remote(msg.at[a], ag.at[a, t], ag_ss.at[a, k], ag_rs.at[a, t], s + 1, dt).start()
-
-        @pl.when(s == last)
+                remote(msg.at[a], ag.at[a, my_j], ag_ss.at[a, k], ag_rs.at[a, my_j],
+                       s + 1, dt).start()
+
+        @pl.when(is_owner & (s == last))
         def _():
             for n in range(sper):
                 ds = a * sper + n
-                send(msg.at[a, :, pl.ds(0, Wp)], fin_p, fp_ss.at[a, n], fp_rs, ds, t)
+                for b in range(per):
+                    send(msg.at[a, :, inside(b)], fin_p, fp_ss.at[a, n * per + b], fp_rs,
+                         ds, my_j * per + b)
                 for b in range(T):
-                    send(msg.at[a, :, pl.ds(Wp, 128)], fin_s.at[t], fs_ss.at[a, n * T + b],
-                         fs_rs.at[t], ds, b)
+                    send(msg.at[a, :, pl.ds(GW, 128)], fin_s.at[my_j], fs_ss.at[a, n * T + b],
+                         fs_rs.at[my_j], ds, b)
 
     for a in range(G):
         enter(a)
@@ -341,7 +329,7 @@
 
     wait(fin_x, fx_rs)
     wait(fin_p, fp_rs)
-    for o in range(T):
+    for o in range(quarters):
         wait(fin_s.at[o], fs_rs.at[o])
     inv = total_of(fin_s, lambda ref, o: ref[o])
     fin_f[...] = fin_x[...].astype(f32) + inv * fin_p[...].astype(f32)
@@ -359,9 +347,8 @@
             wait(resid, xg_ss.at[k])
 
     for a in range(G):
-        for j, outs in targets():
-            for o, k in outs:
-                wait(part.at[a, :, window(o)], rs_ss.at[a, k])
+        for j in range(quarters):
+            sent(part.at[a, j], rs_ss.at[a, j], s, first + j)
 
     @pl.when(s > 0)
     def _():
@@ -372,6 +359,10 @@
     def _():
         for a in range(G):
             wait(x_ref.at[a], xf_ss.at[a])
+
+    @pl.when(is_owner & (s < last))
+    def _():
+        for a in range(G):
             for k in range(T):
                 wait(msg.at[a], ag_ss.at[a, k])
 
@@ -379,11 +370,17 @@
     def _():
         for a in range(G):
             for n in range(sper):
+                sent(x_ref.at[a, :, my_cols], fx_ss.at[a, n], a * sper + n, t)
+
+    @pl.when(is_owner & (s == last))
+    def _():
+        for a in range(G):
+            for n in range(sper):
                 ds = a * sper + n
-                sent(x_ref.at[a, :, my_cols], fx_ss.at[a, n], ds, t)
-                sent(msg.at[a, :, pl.ds(0, Wp)], fp_ss.at[a, n], ds, t)
+                for b in range(per):
+                    sent(msg.at[a, :, inside(b)], fp_ss.at[a, n * per + b], ds, my_j * per + b)
                 for b in range(T):
-                    sent(msg.at[a, :, pl.ds(Wp, 128)], fs_ss.at[a, n * T + b], ds, b)
+                    sent(msg.at[a, :, pl.ds(GW, 128)], fs_ss.at[a, n * T + b], ds, b)
 
 
 def on_device(
@@ -399,6 +396,10 @@
     KL = key_cache.shape[2]
     G = R // BLOCK
     Wp = -(-(D // 128) // T) * 128
+    chunks = D // 128
+    per = next(n for n in range(1, T + 1) if (chunks * n) % T == 0)
+    quarters = T // per
+    GW = chunks * per // T * 128
     sper = BLOCK // rc
     dma = pltpu.SemaphoreType.DMA
     vm = pltpu.VMEM
@@ -416,12 +417,13 @@
         vm((R, (H + 2 * KL) * HD), f32),
         vm((H, BLOCK, HD), f32), vm((KL, BLOCK, HD), f32), vm((KL, BLOCK, HD), f32),
         vm((BLOCK, H * HD), f32),
-        vm((G, BLOCK, D), bf16), vm((G, T, BLOCK, Wp), bf16), vm((G, BLOCK, Wp + 128), bf16),
-        vm((G, T, BLOCK, Wp + 128), bf16), vm((BLOCK, Wp), bf16), vm((BLOCK, Wp), bf16),
-        vm((T, BLOCK, 128), bf16), vm((BLOCK, Wp), f32),
+        vm((G, quarters, BLOCK, GW), bf16), vm((G, T, BLOCK, GW), bf16),
+        vm((G, BLOCK, GW + 128), bf16),
+        vm((G, quarters, BLOCK, GW + 128), bf16), vm((BLOCK, Wp), bf16), vm((BLOCK, Wp), bf16),
+        vm((quarters, BLOCK, 128), bf16), vm((BLOCK, Wp), f32),
         dma((14,)), dma((T,)), dma((S, T)), dma((G,)), dma((G,)), dma((T,)), dma((T,)),
-        dma((G, T)), dma((G, T)), dma((G, T)), dma((G, T)),
-        dma((G, sper)), dma, dma((G, sper)), dma, dma((G, sper * T)), dma((T,)),
+        dma((G, quarters)), dma((G, T)), dma((G, T)), dma((G, quarters)),
+        dma((G, sper)), dma, dma((G, sper * per)), dma, dma((G, sper * T)), dma((quarters,)),
     ]
     return pl.pallas_call(
         functools.partial(kernel, S, T),

time: 73.6 us -> 70.4 us (0.957)
  Pallas kernels: 72 us -> 68.9 us
    pallas_call x1, Pallas kernels: 72 us -> 68.9 us  [on_device(): pl.pallas_call(functools.partial(kernel, S, T), out_shape=jax.ShapeDtypeS...]
where the time goes in v5:
time: 70.4 us; the launch traced here: 70.2 us
  Pallas kernels  68.9 us (98%)
  local copies, waits for them, and re-layouts  1.3 us (2%)
    pallas_call x1, Pallas kernels, on_device(): pl.pallas_call(functools.partial(kernel, S, T), out_shape=jax.ShapeDtypeS...  68.9 us

profile of v5, /device:TPU:5, one launch (start us, length us, event | category | flops | bytes accessed | tf_op | source)
XLA Modules:
  0.0 70.2 jit_solution(11171928053875390192)
XLA Ops:
  0.0 68.9 %shard_map.136 = bf16[8,576]{1,0:T(8,128)(2,1)} custom-call(s32[32]{0:T(128)} %lengths_h.1, s32[32]{0:T(128)} %concept_h.1, s32[32]{0:T(128)} %steer_h.1, f32[32]{0:T(128)} %strength_h.1, bf16[8,576]{1,0:T(8,128)(2,1)} %resid_h.1, f32[1,4608]{1,0:T(1,128)} %pre_h.1, f32[1,4608]{1,0:T(1,128)} %post_h.1, bf16[1,4608,512]{2,1,0:T(8,128)(2,1)} %wq.1, ...), custom_call_target="tpu_custom_call" | custom-call | tf_op jit(solution)/shard_map/pallas_call | solution.py:428
  68.9 1.3 %copy.16 = bf16[8,576]{1,0:T(8,128)(2,1)} copy(bf16[8,576]{1,0:T(8,128)(2,1)} %shard_map.136) | data formatting | bytes 18432

commit v6 on v5

--- a/solution.py
+++ b/solution.py
@@ -170,9 +170,14 @@
 
     for n in (8, 9, 10):
         loads[n].wait()
-    proj[...] = matmul(
-        jnp.concatenate([(base[a] * pre[...]).astype(bf16) for a in range(G)], axis=0),
-        slice(0, D))
+
+    def ahead(j, acc):
+        at = pl.ds(pl.multiple_of(j * GW, 128), GW)
+        known = jnp.concatenate(
+            [(base[a, :, at] * pre[:, at]).astype(bf16) for a in range(G)], axis=0)
+        return acc + matmul(known, at)
+
+    proj[...] = lax.fori_loop(0, quarters, ahead, jnp.zeros(proj.shape, f32))
 
     my_cols = window(t)
     first = T // quarters
@@ -207,13 +212,13 @@
 
         @pl.when(s > 0)
         def _():
-            acc = None
-            for j in range(quarters):
+            def arrive(j, acc):
                 wait(ag.at[a, j], ag_rs.at[a, j])
-                at = slice(j * GW, (j + 1) * GW)
+                at = pl.ds(pl.multiple_of(j * GW, 128), GW)
                 p = ag[a, j, :, 0:GW].astype(f32)
-                term = matmul((p * pre[:, at]).astype(bf16), at)
-                acc = term if acc is None else acc + term
+                return acc + matmul((p * pre[:, at]).astype(bf16), at)
+
+            acc = lax.fori_loop(0, quarters, arrive, jnp.zeros((BLOCK, proj.shape[1]), f32))
             inv = total_of(ag, lambda ref, o: ref[a, o, :, GW:GW + 128])
             for j in range(quarters):
                 at = slice(j * GW, (j + 1) * GW)
@@ -284,10 +289,14 @@
         if a == 0:
             loads[13].wait()
         hb = heads[...].astype(bf16)
-        for j in range(quarters):
-            at = slice(j * GW, (j + 1) * GW)
+
+        def quarter(j, carry):
+            at = pl.ds(pl.multiple_of(j * GW, 128), GW)
             part[a, j] = jnp.dot(hb, wo_v[:, at], preferred_element_type=f32).astype(bf16)
             send(part.at[a, j], rs.at[a, t], rs_ss.at[a, j], rs_rs.at[a, t], s, first + j)
+            return carry
+
+        lax.fori_loop(0, quarters, quarter, 0)
 
     def reduce(a):
         @pl.when(is_owner)
@@ -315,9 +324,13 @@
                 for b in range(per):
                     send(msg.at[a, :, inside(b)], fin_p, fp_ss.at[a, n * per + b], fp_rs,
                          ds, my_j * per + b)
-                for b in range(T):
+
+                def tell(b, carry):
                     send(msg.at[a, :, pl.ds(GW, 128)], fin_s.at[my_j], fs_ss.at[a, n * T + b],
                          fs_rs.at[my_j], ds, b)
+                    return carry
+
+                lax.fori_loop(0, T, tell, 0)
 
     for a in range(G):
         enter(a)

time: 70.4 us -> 73.5 us (1.044)
  Pallas kernels: 68.9 us -> 71.9 us
    pallas_call x1, Pallas kernels: 68.9 us -> 71.9 us  [on_device(): pl.pallas_call(functools.partial(kernel, S, T), out_shape=jax.ShapeDtypeS...]
where the time goes in v6:
time: 73.5 us; the launch traced here: 73.2 us
  Pallas kernels  71.9 us (98%)
  local copies, waits for them, and re-layouts  1.3 us (2%)
    pallas_call x1, Pallas kernels, on_device(): pl.pallas_call(functools.partial(kernel, S, T), out_shape=jax.ShapeDtypeS...  71.9 us

profile of v6, /device:TPU:5, one launch (start us, length us, event | category | flops | bytes accessed | tf_op | source)
XLA Modules:
  0.0 73.2 jit_solution(10810974234861291237)
XLA Ops:
  0.0 71.9 %shard_map.136 = bf16[8,576]{1,0:T(8,128)(2,1)} custom-call(s32[32]{0:T(128)} %lengths_h.1, s32[32]{0:T(128)} %concept_h.1, s32[32]{0:T(128)} %steer_h.1, f32[32]{0:T(128)} %strength_h.1, bf16[8,576]{1,0:T(8,128)(2,1)} %resid_h.1, f32[1,4608]{1,0:T(1,128)} %pre_h.1, f32[1,4608]{1,0:T(1,128)} %post_h.1, bf16[1,4608,512]{2,1,0:T(8,128)(2,1)} %wq.1, ...), custom_call_target="tpu_custom_call" | custom-call | tf_op jit(solution)/shard_map/pallas_call | solution.py:441
  71.9 1.3 %copy.16 = bf16[8,576]{1,0:T(8,128)(2,1)} copy(bf16[8,576]{1,0:T(8,128)(2,1)} %shard_map.136) | data formatting | bytes 18432

commit v7 on v5

--- a/solution.py
+++ b/solution.py
@@ -284,8 +284,9 @@
         if a == 0:
             loads[13].wait()
         hb = heads[...].astype(bf16)
-        for j in range(quarters):
-            at = slice(j * GW, (j + 1) * GW)
+        for i in range(quarters):
+            j = lax.rem(t + i, quarters)
+            at = pl.ds(pl.multiple_of(j * GW, 128), GW)
             part[a, j] = jnp.dot(hb, wo_v[:, at], preferred_element_type=f32).astype(bf16)
             send(part.at[a, j], rs.at[a, t], rs_ss.at[a, j], rs_rs.at[a, t], s, first + j)
 

time: 70.4 us -> 70.8 us (level)
  no operation moved by 1% of the time
where the time goes in v7:
time: 70.8 us; the launch traced here: 70.5 us
  Pallas kernels  69.2 us (98%)
  local copies, waits for them, and re-layouts  1.3 us (2%)
    pallas_call x1, Pallas kernels, on_device(): pl.pallas_call(functools.partial(kernel, S, T), out_shape=jax.ShapeDtypeS...  69.2 us

profile of v7, /device:TPU:5, one launch (start us, length us, event | category | flops | bytes accessed | tf_op | source)
XLA Modules:
  0.0 70.5 jit_solution(6863301373361624669)
XLA Ops:
  0.0 69.2 %shard_map.136 = bf16[8,576]{1,0:T(8,128)(2,1)} custom-call(s32[32]{0:T(128)} %lengths_h.1, s32[32]{0:T(128)} %concept_h.1, s32[32]{0:T(128)} %steer_h.1, f32[32]{0:T(128)} %strength_h.1, bf16[8,576]{1,0:T(8,128)(2,1)} %resid_h.1, f32[1,4608]{1,0:T(1,128)} %pre_h.1, f32[1,4608]{1,0:T(1,128)} %post_h.1, bf16[1,4608,512]{2,1,0:T(8,128)(2,1)} %wq.1, ...), custom_call_target="tpu_custom_call" | custom-call | tf_op jit(solution)/shard_map/pallas_call | solution.py:429
  69.2 1.3 %copy.16 = bf16[8,576]{1,0:T(8,128)(2,1)} copy(bf16[8,576]{1,0:T(8,128)(2,1)} %shard_map.136) | data formatting | bytes 18432
